TPU v7x, 256 devices: a whole 4x4x8 slice. The times are simulated.
256 devices in a mesh: src: 64 (over z, x, core), tgt: 4 (over y).
Axes of the slice: x: 4, y: 4, z: 8, core: 2. Of those that a mesh axis runs over, the one named last changes fastest.
Arguments:
- source_points: float32 [64, 65536], P(None, 'src'), may hold values from -24 to 24
- target_points: float32 [64, 16384], P(None, 'tgt'), may hold values from -24 to 24
- log_source_mass: float32 [65536], P('src'), may hold values from -1 to 1
- log_target_mass: float32 [16384], P('tgt'), may hold values from -1 to 1
Outputs:
- source_potential: float32 [65536], P('src')
- target_potential: float32 [16384], P('tgt')
- source_gradient: float32 [64, 65536], P(None, 'src')
- target_gradient: float32 [64, 4, 4096], P(None, 'tgt', 'src')
All inputs are finite; a program needn't handle non-finite values.
Results may differ from a plain program's by a relative error of at most 0.0003.
Values sent between devices are 32-bit elements; how exact they have to be, the bound alone decides.
A program may use at most 128 MiB of HBM per device.

v0:
```python
import jax
import jax.numpy as jnp
from jax import lax
from jax.sharding import PartitionSpec as P

ITERS = 2


EPSILON = 0.05


def pair_cost(points_a, points_b):
    cross = lax.dot_general(
        points_a,
        points_b,
        (((0,), (0,)), ((), ())),
        precision=lax.Precision.HIGHEST,
        preferred_element_type=jnp.float32,
    )
    norms_a = jnp.sum(points_a * points_a, 0)
    norms_b = jnp.sum(points_b * points_b, 0)
    return (norms_a[:, None] + norms_b[None, :] - 2.0 * cross) / points_a.shape[0]


def row_lse(scores):
    top = lax.pmax(jnp.max(scores, 1), "tgt")
    total = lax.psum(jnp.sum(jnp.exp(scores - top[:, None]), 1), "tgt")
    return top + jnp.log(total)


def column_lse(scores):
    top = lax.pmax(jnp.max(scores, 0), "src")
    total = lax.psum(jnp.sum(jnp.exp(scores - top[None, :]), 0), "src")
    return top + jnp.log(total)


def local(source_points, target_points, log_source_mass, log_target_mass):
    target_pot = jnp.zeros((target_points.shape[1],), jnp.float32)
    source_pot = jnp.zeros((source_points.shape[1],), jnp.float32)
    for step in range(ITERS):
        cost = pair_cost(source_points, target_points)
        source_pot = -EPSILON * row_lse(
            log_target_mass[None, :] + (target_pot[None, :] - cost) / EPSILON
        )
        cost = pair_cost(source_points, target_points)
        target_pot = -EPSILON * column_lse(
            log_source_mass[:, None] + (source_pot[:, None] - cost) / EPSILON
        )
    cost = pair_cost(source_points, target_points)
    plan = jnp.exp(
        log_source_mass[:, None]
        + log_target_mass[None, :]
        + (source_pot[:, None] + target_pot[None, :] - cost) / EPSILON
    )
    moved = lax.dot_general(
        target_points,
        plan,
        (((1,), (1,)), ((), ())),
        precision=lax.Precision.HIGHEST,
        preferred_element_type=jnp.float32,
    )
    source_term = source_points * jnp.sum(plan, 1)[None, :] - moved
    source_grad = lax.psum(source_term, "tgt")
    pulled = lax.dot_general(
        source_points,
        plan,
        (((1,), (0,)), ((), ())),
        precision=lax.Precision.HIGHEST,
        preferred_element_type=jnp.float32,
    )
    target_term = target_points * jnp.sum(plan, 0)[None, :] - pulled
    target_grad = lax.psum_scatter(target_term, "src", scatter_dimension=1, tiled=True)
    return (source_pot, target_pot, source_grad, target_grad[:, None, :])


def solution(mesh):
    placed = (P(None, "src"), P(None, "tgt"), P("src"), P("tgt"))
    return jax.shard_map(
        local,
        mesh=mesh,
        in_specs=placed,
        out_specs=(P("src"), P("tgt"), P(None, "src"), P(None, "tgt", "src")),
        check_vma=False,
    )
```

profile of v0, /device:TPU:1, one launch (start us, length us, event | category | flops | bytes accessed | tf_op | source)
XLA Modules:
  0.0 1286.4 jit_solution(17901619393498821786)
XLA Ops:
  8.0 0.0 reduce-scatter.4.cloned.1.call-start
  8.0 1.0 multiply_reduce_fusion.1
  9.0 1.3 multiply_reduce_fusion
  10.4 0.0 copy-start.3
  10.4 21.3 %fusion = (f32[1024]{0:T(1024)S(1)}, f32[1024,4096]{1,0:T(8,128)}) fusion(f32[4096]{0:T(1024)} %param.7, f32[64,1024]{1,0:T(8,128)} %param.4, f32[64,4096]{1,0:T(8,128)} %param.5, f32[4096]{0:T(1024)S(1)} %multiply_reduce_fusion, f32[1024]{0:T(1024)S(1)} %multiply_reduce_fusion.1), kind=kOutput, calls=%fused_computation.10 | convolution fusion | flops 3254778880 | bytes 18128896 | tf_op jit(solution)/shard_map/dot_general | solution.py:13
  31.7 0.0 copy-start.4
  31.7 9.5 pmax.28
  41.2 0.0 copy-done.3
  41.2 8.1 exponential_reduce_fusion.3
  49.3 6.0 psum.35
  55.3 0.0 copy-done.4
  55.3 9.1 fusion.1
  64.5 248.6 %pmax.29 = f32[4096]{0:T(1024)S(1)} all-reduce(f32[4096]{0:T(1024)S(1)} %fusion.1), channel_id=1, replica_groups=mesh['src'=64,'tgt'=4] {'src'}, use_global_device_ids=true, to_apply=%region_7.0 | all-reduce | flops 4096 | bytes 32768 | tf_op jit(solution)/shard_map/pmax | solution.py:32
  313.1 8.1 exponential_reduce_fusion.2
  321.2 246.6 %psum.36 = f32[4096]{0:T(1024)S(1)} all-reduce(f32[4096]{0:T(1024)S(1)} %exponential_reduce_fusion.2), channel_id=1, replica_groups=mesh['src'=64,'tgt'=4] {'src'}, use_global_device_ids=true, to_apply=%region_9.0 | all-reduce | flops 4096 | bytes 32768 | tf_op jit(solution)/shard_map/psum | solution.py:33
  567.8 8.0 fusion.2
  575.9 7.7 pmax.30
  583.6 8.1 exponential_reduce_fusion.1
  591.8 6.0 psum.37
  597.8 0.0 copy-start.6
  597.8 9.1 fusion.3
  606.9 249.9 %pmax.31 = f32[4096]{0:T(1024)S(1)} all-reduce(f32[4096]{0:T(1024)S(1)} %fusion.3), channel_id=1, replica_groups=mesh['src'=64,'tgt'=4] {'src'}, use_global_device_ids=true, to_apply=%region_15.0 | all-reduce | flops 4096 | bytes 32768 | tf_op jit(solution)/shard_map/pmax | solution.py:32
  856.8 8.1 exponential_reduce_fusion
  864.9 246.3 %psum.38 = f32[4096]{0:T(1024)S(1)} all-reduce(f32[4096]{0:T(1024)S(1)} %exponential_reduce_fusion), channel_id=1, replica_groups=mesh['src'=64,'tgt'=4] {'src'}, use_global_device_ids=true, to_apply=%region_17.0 | all-reduce | flops 4096 | bytes 32768 | tf_op jit(solution)/shard_map/psum | solution.py:33
  1111.3 0.0 copy-done.6
  1111.3 0.0 copy-start.5
  1111.3 0.0 copy-start.1
  1111.3 0.0 copy-start.2
  1111.3 9.3 fusion.6
  1120.6 0.0 copy-done.5
  1120.6 0.0 copy-start
  1120.7 5.7 copy-done
  1126.4 0.0 copy-done.1
  1126.4 0.0 copy-done.2
  1126.4 11.1 fusion.4
  1137.5 2.0 copy.10
  1139.4 0.0 reduce-scatter.4.cloned.1.call-update
  1139.5 0.3 all-reduce.2.cloned.1.call-start
  1139.7 20.5 %fusion.5 = f32[64,1024]{1,0:T(8,128)} fusion(f32[1024,4096]{1,0:T(8,128)} %copy-done, f32[64,4096]{1,0:T(8,128)S(1)} %copy-done.1, f32[64,1024]{1,0:T(8,128)S(1)} %copy-done.2, f32[1024]{0:T(1024)S(1)} %get-tuple-element.13), kind=kOutput, calls=%fused_computation.17 | convolution fusion | flops 3221356544 | bytes 18354176 | tf_op jit(solution)/shard_map/dot_general | solution.py:55
  1160.2 0.0 all-reduce.2.cloned.1.call-update
  1160.2 115.4 %reduce-scatter.4.cloned.1.call-done = f32[64,64]{1,0:T(8,128)} async-done(((f32[4096,64]{1,0:T(8,128)}), f32[64,64]{1,0:T(8,128)}) %reduce-scatter.4.cloned.1.call-update) | async-done | bytes 16400
  1275.6 1.5 copy.11
  1277.1 0.0 all-reduce.2.cloned.1.call-done
  1277.1 1.7 copy.13
  (4 shorter events, 0.0 us)
Async XLA Ops:
  8.0 1267.6 %reduce-scatter.4.cloned.1.call-start = ((), (), s32[]{:S(2)}) async-start(), calls=%async_computation.2 | async-start | bytes 2129920
  10.4 30.9 %copy-start.3 = (f32[4096]{0:T(1024)S(1)}, f32[4096]{0:T(1024)}, u32[]{:S(2)}) copy-start(f32[4096]{0:T(1024)} %param.7) | copy-start | bytes 49156
  31.7 23.7 %copy-start.4 = (f32[1024]{0:T(1024)S(1)}, f32[1024]{0:T(1024)}, u32[]{:S(2)}) copy-start(f32[1024]{0:T(1024)} %param.6) | copy-start | bytes 12292
  597.8 513.5 %copy-start.6 = (f32[1024]{0:T(1024)}, f32[1024]{0:T(1024)S(1)}, u32[]{:S(2)}) copy-start(f32[1024]{0:T(1024)S(1)} %add_multiply_fusion.2) | copy-start | bytes 12292
  1111.3 9.4 copy-start.5
  1111.3 15.1 %copy-start.1 = (f32[64,4096]{1,0:T(8,128)S(1)}, f32[64,4096]{1,0:T(8,128)}, u32[]{:S(2)}) copy-start(f32[64,4096]{1,0:T(8,128)} %param.5) | copy-start | bytes 3145732
  1111.3 15.1 %copy-start.2 = (f32[64,1024]{1,0:T(8,128)S(1)}, f32[64,1024]{1,0:T(8,128)}, u32[]{:S(2)}) copy-start(f32[64,1024]{1,0:T(8,128)} %param.4) | copy-start | bytes 786436
  1120.6 5.7 copy-start
  1139.5 137.6 %all-reduce.2.cloned.1.call-start = ((), (), s32[]{:S(2)}) async-start(), calls=%async_computation.1 | async-start | bytes 524288 | tf_op jit(solution)/shard_map/psum | solution.py:63
Sparse Core Ops, SparseCore 0:
  1139.6 135.9 reduce-scatter.3
Sparse Core Ops, SparseCore 1:
  1160.3 45.4 all-reduce.1
where the time goes:
time: 1300 us; the launch traced here: 1290 us
  blocking collectives  1020 us (78%)
  waiting for transfers between devices  115 us (9%)
  other arithmetic  70.4 us (5%)
  matrix products  52.9 us (4%)
  between operations  15.8 us (1%)
    pmax x2, blocking collectives, column_lse(): top = lax.pmax(jnp.max(scores, 0), 'src')  499 us
    psum x2, blocking collectives, column_lse(): total = lax.psum(jnp.sum(jnp.exp(scores - top[None, :]), 0), 'src')  493 us
    unnamed x3, waiting for transfers between devices  115 us
  transfers between devices with their start and end apart: 2, of which 1 were waited for; matrix products, arithmetic and copies ran while one was open for 2% of the time, Pallas kernels for 0%

commit v1 on v0

v1 whole, which is shorter than its diff:
```python
import functools

import jax
import jax.numpy as jnp
import numpy as np
from jax import lax
from jax.experimental import pallas as pl
from jax.experimental.pallas import tpu as pltpu
from jax.sharding import PartitionSpec as P

EPSILON = 0.05
LOG2E = float(np.log2(np.e))
BETA = LOG2E / EPSILON
MESH = pl.DeviceIdType.MESH
F32 = jnp.float32
BF16 = jnp.bfloat16


def split3(a):
    hi = a.astype(BF16)
    rest = a - hi.astype(F32)
    mid = rest.astype(BF16)
    lo = (rest - mid.astype(F32)).astype(BF16)
    return hi, mid, lo


class Exchange:
    def __init__(self, sems, me, n, device):
        self.send, self.recv, self.base = sems
        self.me, self.n, self.device = me, n, device

    def copy(self, r, src, dst):
        peer = lax.rem(self.me + r, self.n)
        return pltpu.make_async_remote_copy(
            src_ref=src(peer),
            dst_ref=dst(self.me),
            send_sem=self.send.at[self.base + r - 1],
            recv_sem=self.recv.at[self.base + r - 1],
            device_id=self.device(peer),
            device_id_type=MESH,
        )

    def start(self, src, dst):
        self.copies = [self.copy(r, src, dst) for r in range(1, self.n)]
        for copy in self.copies:
            copy.start()

    def wait_recv(self):
        for copy in self.copies:
            copy.wait_recv()

    def wait_send(self):
        for copy in self.copies:
            copy.wait_send()


def kernel(dims, x_ref, y_ref, la_ref, lb_ref,
           f_out, g_out, sg_out, tg_out,
           p_ref, hi_ref, lo_ref, xk_ref, yk_ref, mx_ref, sm_ref, vb_ref,
           fm_ref, fr_ref, mg_ref, ga_ref, gb_ref, gf_ref, w_ref, k_ref,
           ca_ref, cs_ref, cb_ref, d_ref, a_ref, xa_ref, yb_ref,
           u_ref, r0_ref, t1_ref, r1_ref, t2_ref, r2_ref, r3_ref,
           so_ref, sr_ref, sgb_ref, send_sems, recv_sems):
    NX, NZ, NY = dims
    NQ = 2 * NX
    E, S = x_ref.shape
    T = y_ref.shape[1]
    CB = T // NZ
    RB = S // NY
    TB = CB // 128
    NT = T // 128
    RS = 128

    src = lax.axis_index("src")
    me_y = lax.axis_index("tgt")
    me_z = src // NQ
    me_q = lax.rem(src, NQ)
    me_x = me_q // 2
    me_c = lax.rem(me_q, 2)

    dev_y = lambda j: {"tgt": j}
    dev_z = lambda j: {"src": j * NQ + me_q}
    dev_q = lambda j: {"src": me_z * NQ + j}
    dev_x = lambda j: {"src": me_z * NQ + j * 2 + me_c}
    dev_c = lambda j: {"src": me_z * NQ + me_x * 2 + j}

    taken = [0]

    def group(me, n, device):
        base = taken[0]
        taken[0] += n - 1
        return Exchange((send_sems, recv_sems, base), me, n, device)

    barrier = pltpu.get_barrier_semaphore()
    partners = 0
    for me, n, device in ((me_y, NY, dev_y), (me_z, NZ, dev_z), (me_q, NQ, dev_q)):
        for r in range(1, n):
            pl.semaphore_signal(barrier, inc=1, device_id=device(lax.rem(me + r, n)), device_id_type=MESH)
            partners += 1

    def prep_y(b, _):
        cols = pl.ds(pl.multiple_of(b * CB, CB), CB)
        y = y_ref[:, cols]
        y1, y2, y3 = split3(y)
        for n, part in enumerate((y1, y2, y1, y3, y2, y1)):
            yk_ref[n * E:(n + 1) * E, cols] = part
        u = LOG2E * lb_ref[:, cols] - (BETA / E) * jnp.sum(y * y, 0, keepdims=True)
        u1, u2, u3 = split3(u)
        row = lax.broadcasted_iota(jnp.int32, (16, CB), 0)
        pick = lambda n, v: jnp.where(row == n, jnp.broadcast_to(v.astype(F32), (16, CB)), 0.0)
        yk_ref[6 * E:6 * E + 16, cols] = (pick(0, u1) + pick(1, u2) + pick(2, u3)).astype(BF16)
        yk_ref[6 * E + 16:8 * E, cols] = jnp.zeros((2 * E - 16, CB), BF16)
        return 0

    lax.fori_loop(0, NZ, prep_y, 0)

    lane = lax.broadcasted_iota(jnp.int32, (128, 128), 1)
    left = lane < E

    def prep_x(i, _):
        rows = pl.ds(pl.multiple_of(i * 128, 128), 128)
        x = x_ref[:, rows] * (2.0 * BETA / E)
        x1, x2, x3 = (v.astype(F32) for v in split3(jnp.concatenate([x, x], 0).T))
        xk_ref[rows, 0:128] = x1.astype(BF16)
        xk_ref[rows, 128:256] = jnp.where(left, x2, x1).astype(BF16)
        xk_ref[rows, 256:384] = jnp.where(left, x2, x3).astype(BF16)
        xk_ref[rows, 384:512] = jnp.where(lane < 3, 1.0, 0.0).astype(BF16)
        mx_ref[rows, :] = jnp.full((128, 128), -3e38, F32)
        return 0

    lax.fori_loop(0, S // 128, prep_x, 0)

    def scores(b, _):
        cols = pl.ds(pl.multiple_of(b * CB, CB), CB)
        yk = yk_ref[:, cols]
        for i in range(S // RS):
            rows = slice(i * RS, (i + 1) * RS)
            s = jnp.dot(xk_ref[rows, :], yk, preferred_element_type=F32)
            p_ref[rows, cols] = s
            m = mx_ref[rows, :]
            for t in range(TB):
                m = jnp.maximum(m, s[:, t * 128:(t + 1) * 128])
            mx_ref[rows, :] = m
        return 0

    lax.fori_loop(0, NZ, scores, 0)

    def row_sums(i, _):
        rows = pl.ds(pl.multiple_of(i * 16, 16), 16)
        m = mx_ref[rows, :]
        acc = [jnp.zeros((16, 128), F32) for _ in range(2)]
        for t in range(NT):
            acc[t % 2] += jnp.exp2(p_ref[rows, t * 128:(t + 1) * 128] - m)
        sm_ref[rows, :] = acc[0] + acc[1]
        return 0

    lax.fori_loop(0, S // 16, row_sums, 0)

    for i in range(S // 128):
        rows = slice(i * 128, (i + 1) * 128)
        m = mx_ref[rows, :].T
        top = jnp.max(m, 0, keepdims=True)
        total = jnp.sum(sm_ref[rows, :].T * jnp.exp2(m - top), 0, keepdims=True)
        fm_ref[me_y, 0:1, rows] = top
        fm_ref[me_y, 1:2, rows] = total

    pl.semaphore_wait(barrier, partners)
    f1 = group(me_y, NY, dev_y)
    f1.start(lambda peer: fm_ref.at[me_y], lambda me: fm_ref.at[me])
    f1.wait_recv()

    def combine(ref, n):
        top = ref[0, 0:1, :]
        for j in range(1, n):
            top = jnp.maximum(top, ref[j, 0:1, :])
        total = ref[0, 1:2, :] * jnp.exp2(ref[0, 0:1, :] - top)
        for j in range(1, n):
            total = total + ref[j, 1:2, :] * jnp.exp2(ref[j, 0:1, :] - top)
        return top, total

    def add_up(ref, n):
        total = ref[0]
        for j in range(1, n):
            total = total + ref[j]
        return total

    def spread(row):
        for i in range(S // 128):
            part = row[:, i * 128:(i + 1) * 128]
            vb_ref[i * 128:(i + 1) * 128, :] = jnp.broadcast_to(part, (128, 128)).T

    top, total = combine(fm_ref, NY)
    lse = top + jnp.log2(total)
    la2 = LOG2E * la_ref[...]
    spread(la2 - lse)

    def columns(b, _):
        cols = pl.ds(pl.multiple_of(b * CB, CB), CB)

        def scored(i):
            rows = pl.ds(pl.multiple_of(i * RS, RS), RS)
            v = vb_ref[rows, :]
            return p_ref[rows, cols] + jnp.concatenate([v] * TB, 1)

        def find(i, m):
            return jnp.maximum(m, jnp.max(scored(i).reshape(RS // 8, 8, CB), 0))

        m = lax.fori_loop(0, S // RS, find, jnp.full((8, CB), -3e38, F32))
        m = jnp.max(m, 0, keepdims=True)

        def weigh(i, acc):
            rows = pl.ds(pl.multiple_of(i * RS, RS), RS)
            e = jnp.exp2(scored(i) - m)
            p_ref[rows, cols] = e
            return acc + jnp.sum(e.reshape(RS // 8, 8, CB), 0)

        acc = lax.fori_loop(0, S // RS, weigh, jnp.zeros((8, CB), F32))
        mg_ref[b, 0:1, :] = m
        mg_ref[b, 1:2, :] = jnp.sum(acc, 0, keepdims=True)
        return 0

    lax.fori_loop(0, NZ, columns, 0)

    gA = group(me_q, NQ, dev_q)
    gA.start(lambda peer: mg_ref.at[peer], lambda me: ga_ref.at[me])
    ga_ref[me_q] = mg_ref[me_q]

    def split_rows(first, last):
        def body(i, _):
            rows = pl.ds(pl.multiple_of(i * 16, 16), 16)
            for t in range(NT // 4):
                lanes = slice(t * 512, (t + 1) * 512)
                e = p_ref[rows, lanes]
                hi = e.astype(BF16)
                hi_ref[rows, lanes] = hi
                lo_ref[rows, lanes] = (e - hi.astype(F32)).astype(BF16)
            return 0

        lax.fori_loop(first, last, body, 0)

    strips = S // 16
    split_rows(0, strips // 3)
    gA.wait_recv()
    top, total = combine(ga_ref, NQ)
    gb_ref[me_z, 0:1, :] = top
    gb_ref[me_z, 1:2, :] = total
    gB = group(me_z, NZ, dev_z)
    gB.start(lambda peer: gb_ref.at[me_z], lambda me: gb_ref.at[me])
    split_rows(strips // 3, 2 * strips // 3)
    gB.wait_recv()
    top, total = combine(gb_ref, NZ)
    gf_ref[me_q] = top + jnp.log2(total)
    gC = group(me_q, NQ, dev_q)
    gC.start(lambda peer: gf_ref.at[me_q], lambda me: gf_ref.at[me])
    split_rows(2 * strips // 3, strips)
    gC.wait_recv()

    for b in range(NZ):
        k = jnp.exp2(mg_ref[b, 0:1, :] - gf_ref[b])
        k_ref[b] = k
        w_ref[b] = k * jnp.exp(lb_ref[:, b * CB:(b + 1) * CB])

    def row_dots(i, _):
        rows = pl.ds(pl.multiple_of(i * 64, 64), 64)
        acc = jnp.zeros((64, 128), F32)
        for t in range(NT):
            w = w_ref[t // TB, :, (t % TB) * 128:(t % TB + 1) * 128]
            acc += p_ref[rows, t * 128:(t + 1) * 128] * w
        sm_ref[rows, :] = acc
        return 0

    lax.fori_loop(0, S // 64, row_dots, 0)
    for i in range(S // 128):
        rows = slice(i * 128, (i + 1) * 128)
        fr_ref[me_y, :, rows] = jnp.sum(sm_ref[rows, :].T, 0, keepdims=True)
    f2 = group(me_y, NY, dev_y)
    f2.start(lambda peer: fr_ref.at[me_y], lambda me: fr_ref.at[me])
    f2.wait_recv()
    total = add_up(fr_ref, NY)
    scale = jnp.exp(la_ref[...]) / total
    spread(scale)
    x = x_ref[...]
    f_out[...] = jnp.sum(x * x, 0, keepdims=True) / E - (jnp.log2(total) - la2 + lse) / BETA
    for k in range(NY):
        a_ref[k] = scale[:, k * RB:(k + 1) * RB]

    def column_dots(b, _):
        cols = pl.ds(pl.multiple_of(b * CB, CB), CB)

        def step(i, acc):
            rows = pl.ds(pl.multiple_of(i * RS, RS), RS)
            v = jnp.concatenate([vb_ref[rows, :]] * TB, 1)
            return acc + jnp.sum((p_ref[rows, cols] * v).reshape(RS // 8, 8, CB), 0)

        acc = lax.fori_loop(0, S // RS, step, jnp.zeros((8, CB), F32))
        cs_ref[b] = jnp.sum(acc, 0, keepdims=True) * k_ref[b]
        return 0

    lax.fori_loop(0, NZ, column_dots, 0)

    cA = group(me_q, NQ, dev_q)
    cA.start(lambda peer: cs_ref.at[peer], lambda me: ca_ref.at[me])
    ca_ref[me_q] = cs_ref[me_q]

    x1, x2, x3 = split3(x * scale)
    xa_ref[0:E, :] = x1
    xa_ref[E:2 * E, :] = x2
    xa_ref[2 * E:3 * E, :] = x3

    def pulled(first, last):
        def body(b, _):
            cols = pl.ds(pl.multiple_of(b * CB, CB), CB)
            xa = xa_ref[...]
            out = jnp.dot(xa, hi_ref[:, cols], preferred_element_type=F32)
            out = out + jnp.dot(xa, lo_ref[:, cols], preferred_element_type=F32)
            out = (out[0:E] + out[E:2 * E] + out[2 * E:3 * E]) * k_ref[b]
            for t in range(NX):
                for h in range(2):
                    u_ref[t, h, b] = out[h * (E // 2):(h + 1) * (E // 2), t * 128:(t + 1) * 128]
            return 0

        lax.fori_loop(first, last, body, 0)

    pulled(0, NZ // 2)
    cA.wait_recv()
    cb_ref[me_z] = add_up(ca_ref, NQ)
    cB = group(me_z, NZ, dev_z)
    cB.start(lambda peer: cb_ref.at[me_z], lambda me: cb_ref.at[me])
    pulled(NZ // 2, NZ)
    cB.wait_recv()
    d_ref[me_q] = add_up(cb_ref, NZ)
    cC = group(me_q, NQ, dev_q)
    cC.start(lambda peer: d_ref.at[me_q], lambda me: d_ref.at[me])
    u0 = group(me_c, 2, dev_c)
    u0.start(lambda peer: u_ref.at[:, peer], lambda me: r0_ref)
    cC.wait_recv()

    def prep_b(b, _):
        cols = pl.ds(pl.multiple_of(b * CB, CB), CB)
        scale_b = w_ref[b] / d_ref[b]
        y1, y2, y3 = split3(y_ref[:, cols] * scale_b)
        yb_ref[0:E, cols] = y1
        yb_ref[E:2 * E, cols] = y2
        yb_ref[2 * E:3 * E, cols] = y3
        b1, b2, b3 = split3(scale_b)
        row = lax.broadcasted_iota(jnp.int32, (E, CB), 0)
        pick = lambda n, v: jnp.where(row == n, jnp.broadcast_to(v.astype(F32), (E, CB)), 0.0)
        yb_ref[3 * E:4 * E, cols] = (pick(0, b1) + pick(1, b2) + pick(2, b3)).astype(BF16)
        return 0

    lax.fori_loop(0, NZ, prep_b, 0)

    u0.wait_recv()
    for t in range(NX):
        t1_ref[t] = u_ref[t, me_c] + r0_ref[t]
    u1 = group(me_x, NX, dev_x)
    u1.start(lambda peer: t1_ref.at[peer], lambda me: r1_ref.at[me])
    r1_ref[me_x] = t1_ref[me_x]

    sg = group(me_y, NY, dev_y)

    def sg_copy(r):
        return pltpu.make_async_remote_copy(
            src_ref=so_ref.at[r],
            dst_ref=sr_ref.at[me_y],
            send_sem=send_sems.at[sg.base + r],
            recv_sem=recv_sems.at[sg.base + r],
            device_id=dev_y(lax.rem(me_y + 1 + r, NY)),
            device_id_type=MESH,
        )

    def moved(r, _):
        k = lax.rem(me_y + 1 + r, NY)
        rows = pl.ds(pl.multiple_of(k * RB, RB), RB)
        nt = (((1,), (1,)), ((), ()))
        yb = yb_ref[...]
        out = lax.dot_general(hi_ref[rows, :], yb, nt, preferred_element_type=F32)
        out = out + lax.dot_general(lo_ref[rows, :], yb, nt, preferred_element_type=F32)
        out = out.T
        mass = out[3 * E:3 * E + 1] + out[3 * E + 1:3 * E + 2] + out[3 * E + 2:3 * E + 3]
        term = x_ref[:, rows] * mass - (out[0:E] + out[E:2 * E] + out[2 * E:3 * E])
        term = term * a_ref[k]

        @pl.when(r < NY - 1)
        def _():
            so_ref[r] = term
            sg_copy(r).start()

        @pl.when(r == NY - 1)
        def _():
            sr_ref[me_y] = term

        return 0

    lax.fori_loop(0, NY, moved, 0)

    u1.wait_recv()
    for j in range(NZ):
        t2_ref[j] = add_up(r1_ref.at[:, j], NX)
    u2 = group(me_z, NZ, dev_z)
    u2.start(lambda peer: t2_ref.at[peer], lambda me: r2_ref.at[me])
    r2_ref[me_z] = t2_ref[me_z]

    for r in range(NY - 1):
        sg_copy(r).wait_recv()
    sgb_ref[me_y] = add_up(sr_ref, NY)
    ag = group(me_y, NY, dev_y)
    ag.start(lambda peer: sgb_ref.at[me_y], lambda me: sgb_ref.at[me])

    u2.wait_recv()
    r3_ref[me_c] = add_up(r2_ref, NZ)
    u3 = group(me_c, 2, dev_c)
    u3.start(lambda peer: r3_ref.at[me_c], lambda me: r3_ref.at[me])

    for b in range(NZ):
        cols = slice(b * CB, (b + 1) * CB)
        g_out[:, cols] = (LOG2E * lb_ref[:, cols] - gf_ref[b] - jnp.log2(d_ref[b])) / BETA

    u3.wait_recv()
    mine = pl.ds(pl.multiple_of((src // 2) * 128, 128), 128)
    d = d_ref[me_z, :, pl.ds(pl.multiple_of(me_x * 128, 128), 128)]
    total = jnp.concatenate([r3_ref[0], r3_ref[1]], 0)
    term = jnp.exp(lb_ref[:, mine]) * (y_ref[:, mine] - total / d)
    tg_out[...] = jnp.where(me_c == 0, term[:, 0:64], term[:, 64:128])

    ag.wait_recv()
    for k in range(NY):
        sg_out[:, k * RB:(k + 1) * RB] = sgb_ref[k]

    for exchange in (f1, gA, gB, gC, f2, cA, cB, cC, u0, u1, u2, ag, u3):
        exchange.wait_send()
    for r in range(NY - 1):
        sg_copy(r).wait_send()


def local(dims, x, y, la, lb):
    NX, NZ, NY = dims
    NQ = 2 * NX
    E, S = x.shape
    T = y.shape[1]
    CB = T // NZ
    RB = S // NY
    n_sems = 3 * (NY - 1) + 4 * (NQ - 1) + 2 * (NZ - 1) + (NY - 1) + 2 + (NX - 1) + (NZ - 1)
    H = E // 2
    vmem = lambda shape, dtype=F32: pltpu.VMEM(shape, dtype)
    out = pl.pallas_call(
        functools.partial(kernel, dims),
        out_shape=(
            jax.ShapeDtypeStruct((1, S), F32),
            jax.ShapeDtypeStruct((1, T), F32),
            jax.ShapeDtypeStruct((E, S), F32),
            jax.ShapeDtypeStruct((E, 64), F32),
        ),
        in_specs=[pl.BlockSpec(memory_space=pltpu.VMEM)] * 4,
        out_specs=[pl.BlockSpec(memory_space=pltpu.VMEM)] * 4,
        scratch_shapes=[
            vmem((S, T)), vmem((S, T), BF16), vmem((S, T), BF16),
            vmem((S, 8 * E), BF16), vmem((8 * E, T), BF16),
            vmem((S, 128)), vmem((S, 128)), vmem((S, 128)),
            vmem((NY, 2, S)), vmem((NY, 1, S)),
            vmem((NQ, 2, CB)), vmem((NQ, 2, CB)), vmem((NZ, 2, CB)), vmem((NQ, 1, CB)),
            vmem((NQ, 1, CB)), vmem((NQ, 1, CB)),
            vmem((NQ, 1, CB)), vmem((NQ, 1, CB)), vmem((NZ, 1, CB)), vmem((NQ, 1, CB)),
            vmem((NY, 1, RB)), vmem((3 * E, S), BF16), vmem((4 * E, T), BF16),
            vmem((NX, 2, NZ, H, 128)), vmem((NX, NZ, H, 128)), vmem((NX, NZ, H, 128)),
            vmem((NX, NZ, H, 128)), vmem((NZ, H, 128)), vmem((NZ, H, 128)), vmem((2, H, 128)),
            vmem((NY - 1, E, RB)), vmem((NY, E, RB)), vmem((NY, E, RB)),
            pltpu.SemaphoreType.DMA((n_sems,)), pltpu.SemaphoreType.DMA((n_sems,)),
        ],
        compiler_params=pltpu.CompilerParams(
            collective_id=0, has_side_effects=True, vmem_limit_bytes=56 * 1024 * 1024
        ),
        cost_estimate=pl.CostEstimate(
            flops=2 * S * T * (8 + 8 + 8) * E, bytes_accessed=4 * (E * (S + T) * 2), transcendentals=2 * S * T
        ),
        name="sinkhorn",
    )(x, y, la[None, :], lb[None, :])
    f, g, sg, tg = out
    return f[0], g[0], sg, tg[:, None, :]


def solution(mesh):
    n_src, n_tgt = mesh.shape["src"], mesh.shape["tgt"]
    n_x = int(round((n_src // 4) ** 0.5))
    dims = (n_x, n_src // (2 * n_x), n_tgt)
    placed = (P(None, "src"), P(None, "tgt"), P("src"), P("tgt"))
    return jax.shard_map(
        functools.partial(local, dims),
        mesh=mesh,
        in_specs=placed,
        out_specs=(P("src"), P("tgt"), P(None, "src"), P(None, "tgt", "src")),
        check_vma=False,
    )
```

time: 1300 us -> 82.1 us (0.06); the launches traced: 1290 us -> 82 us
  blocking collectives: 1020 us -> 0 us
  waiting for transfers between devices: 115 us -> 0 us
  Pallas kernels: 0 us -> 77.1 us
  other arithmetic: 70.4 us -> 0 us
  matrix products: 52.9 us -> 0 us
  between operations: 15.8 us -> 0.65 us
    pmax x4 -> x0, blocking collectives: 516 us -> none  [the longest x2 499 us: column_lse(): top = lax.pmax(jnp.max(scores, 0), 'src')]
    psum x4 -> x0, blocking collectives: 505 us -> none  [the longest x2 493 us: column_lse(): total = lax.psum(jnp.sum(jnp.exp(scores - top[None, :]), 0), 'src')]
    unnamed x3 -> x0, waiting for transfers between devices: 115 us -> none
    pallas_call x0 -> x1, Pallas kernels: none -> 77.1 us  [local(): pl.pallas_call(functools.partial(kernel, dims), out_shape=(jax.ShapeDtype...]
    dot_general x3 -> x0, matrix products: 52.9 us -> none  [the longest x1 21.3 us: pair_cost(): lax.dot_general(points_a, points_b, (((0,), (0,)), ((), ())), precision=l...]
    reduce_sum x7 -> x0, other arithmetic: 44.1 us -> none  [the longest x2 16.2 us: row_lse(): total = lax.psum(jnp.sum(jnp.exp(scores - top[:, None]), 1), 'tgt')]
    reduce_max x3 -> x0, other arithmetic: 26.3 us -> none  [the longest x2 18.3 us: column_lse(): top = lax.pmax(jnp.max(scores, 0), 'src')]
  transfers between devices with their start and end apart: 2 -> 0, of which waited for: 1 -> 0; matrix products, arithmetic and copies ran while one was open for 2% -> 0% of each run, Pallas kernels for 0% -> 0%
where the time goes in v1:
time: 82.1 us; the launch traced here: 82 us
  Pallas kernels  77.1 us (94%)
  local copies, waits for them, and re-layouts  4.18 us (5%)
    pallas_call x1, Pallas kernels, local(): pl.pallas_call(functools.partial(kernel, dims), out_shape=(jax.ShapeDtype...  77.1 us
    unnamed x8, local copies, waits for them, and re-layouts  4.18 us

profile of v1, /device:TPU:1, one launch (start us, length us, event | category | flops | bytes accessed | tf_op | source)
XLA Modules:
  0.0 82.0 jit_solution(17326834169951656448)
XLA Ops:
  0.6 77.1 %sinkhorn.1 = (f32[1,1024]{1,0:T(1,128)}, f32[1,4096]{1,0:T(1,128)}, f32[64,1024]{1,0:T(8,128)}, f32[64,64]{1,0:T(8,128)}) custom-call(f32[64,1024]{1,0:T(8,128)} %x_ref.1, f32[64,4096]{1,0:T(8,128)} %y_ref.1, f32[1,1024]{1,0:T(1,128)} %bitcast.11, f32[1,4096]{1,0:T(1,128)} %bitcast.10), custom_call_target="tpu_custom_call" | custom-call | flops 12884901888 | bytes 2621440 | tf_op jit(solution)/shard_map/sinkhorn/pallas_call | solution.py:446
  77.8 0.0 copy-start.1
  77.8 1.3 %copy.13 = f32[1024]{0:T(1024)} copy(f32[1024]{0:T(1024)} %bitcast.9) | data formatting | bytes 8192
  79.0 0.0 copy-done.1
  79.0 0.6 copy.14
  79.7 0.0 copy-start
  79.7 1.7 %copy.15 = f32[64,1024]{1,0:T(8,128)} copy(f32[64,1024]{1,0:T(8,128)} %get-tuple-element.22) | data formatting | bytes 524288
  81.3 0.0 copy-done
  81.3 0.6 copy.16
Async XLA Ops:
  77.8 1.3 %copy-start.1 = (f32[1,4096]{1,0:T(1,128)S(1)}, f32[1,4096]{1,0:T(1,128)}, u32[]{:S(2)}) copy-start(f32[1,4096]{1,0:T(1,128)} %get-tuple-element.9) | copy-start | bytes 49156
  79.7 1.7 %copy-start = (f32[64,64]{1,0:T(8,128)S(1)}, f32[64,64]{1,0:T(8,128)}, u32[]{:S(2)}) copy-start(f32[64,64]{1,0:T(8,128)} %get-tuple-element.11) | copy-start | bytes 49156

commit v2 on v0

v2 whole, which is shorter than its diff:
```python
import functools

import jax
import jax.numpy as jnp
import numpy as np
from jax import lax
from jax.experimental import pallas as pl
from jax.experimental.pallas import tpu as pltpu
from jax.sharding import PartitionSpec as P

EPSILON = 0.05
LOG2E = float(np.log2(np.e))
BETA = LOG2E / EPSILON
MESH = pl.DeviceIdType.MESH
F32 = jnp.float32
BF16 = jnp.bfloat16
RS = 128
RC = 64
L = 128


def split3(a):
    hi = a.astype(BF16)
    rest = a - hi.astype(F32)
    mid = rest.astype(BF16)
    lo = (rest - mid.astype(F32)).astype(BF16)
    return hi, mid, lo


def ds(start, size):
    return pl.ds(pl.multiple_of(start, size), size)


def lse2(ref, n):
    top = ref[0]
    for j in range(1, n):
        top = jnp.maximum(top, ref[j])
    total = jnp.exp2(ref[0] - top)
    for j in range(1, n):
        total = total + jnp.exp2(ref[j] - top)
    return top + jnp.log2(total)


def add_up(ref, n):
    total = ref[0]
    for j in range(1, n):
        total = total + ref[j]
    return total


class Sends:
    def __init__(self, send_sems, recv_sems):
        self.send_sems, self.recv_sems = send_sems, recv_sems
        self.taken = 0
        self.live = []

    def reserve(self, n):
        self.taken += n
        return self.taken - n

    def copy(self, src, dst, send, recv, device):
        return pltpu.make_async_remote_copy(
            src_ref=src,
            dst_ref=dst,
            send_sem=self.send_sems.at[send],
            recv_sem=self.recv_sems.at[recv],
            device_id=device,
            device_id_type=MESH,
        )

    def exchange(self, src, dst, me, n, device):
        base = self.reserve(n - 1)
        copies = []
        for r in range(1, n):
            peer = lax.rem(me + r, n)
            copies.append(self.copy(src(peer), dst, base + r - 1, base + r - 1, device(peer)))
        for copy in copies:
            copy.start()
        self.live += copies
        return copies


def arrived(copies):
    for copy in copies:
        copy.wait_recv()


def kernel(dims, x_ref, y_ref, la_ref, lb_ref,
           f_out, g_out, sg_out, tg_out,
           p_ref, hi_ref, lo_ref, xk_ref, yk_ref, mx_ref, sm_ref, vb_ref, cm_ref, mf_ref,
           xs_ref, las_ref, tmp_ref, fm_ref, fr_ref, gm_ref, gx_ref, gz_ref, k_ref, w_ref,
           a_ref, xa_ref, yb_ref, cx_ref, cz_ref, d_ref, gs_ref,
           u_ref, r1_ref, t2_ref, r2_ref, tile_ref, so_ref, sc_ref, sy_ref, sr_ref, sgb_ref,
           send_sems, recv_sems):
    NX, NZ, NY = dims
    NQ = 2 * NX
    E, S = x_ref.shape
    T = y_ref.shape[1]
    T2, S2 = T // 2, 2 * S
    HZ = NZ // 2
    CB = NX * L
    RB = S // NY
    NH = NY // 2
    NT, NR, SR = T2 // L, S2 // L, S // L

    src = lax.axis_index("src")
    me_y = lax.axis_index("tgt")
    me_z = src // NQ
    me_q = lax.rem(src, NQ)
    me_x = me_q // 2
    me_c = lax.rem(me_q, 2)
    other = 1 - me_c
    me_f = me_y * 2 + me_c
    chip = src - me_c

    dev_f = lambda j: {"src": chip + lax.rem(j, 2), "tgt": j // 2}
    dev_y = lambda j: {"tgt": j}
    dev_z = lambda j: {"src": j * NQ + me_q}
    dev_x = lambda j: {"src": me_z * NQ + j * 2 + me_c}
    partner = {"src": chip + other}

    sends = Sends(send_sems, recv_sems)
    exchange = sends.exchange

    barrier = pltpu.get_barrier_semaphore()
    greeted = 0
    for me, n, device in ((me_f, 2 * NY, dev_f), (me_x, NX, dev_x), (me_z, NZ, dev_z)):
        for r in range(1, n):
            pl.semaphore_signal(barrier, inc=1, device_id=device(lax.rem(me + r, n)), device_id_type=MESH)
            greeted += 1

    def prep_y(b, _):
        cols = ds(b * CB, CB)
        y = y_ref[:, ds(me_c * T2 + b * CB, CB)]
        y1, y2, y3 = split3(y)
        for n, part in enumerate((y1, y2, y1, y3, y2, y1)):
            yk_ref[n * E:(n + 1) * E, cols] = part
        lb = jnp.concatenate([lb_ref[pl.ds(me_c * NT + b * NX + t, 1), :] for t in range(NX)], 1)
        u = LOG2E * lb - (BETA / E) * jnp.sum(y * y, 0, keepdims=True)
        u1, u2, u3 = split3(u)
        row = lax.broadcasted_iota(jnp.int32, (16, CB), 0)
        pick = lambda n, v: jnp.where(row == n, jnp.broadcast_to(v.astype(F32), (16, CB)), 0.0)
        yk_ref[6 * E:6 * E + 16, cols] = (pick(0, u1) + pick(1, u2) + pick(2, u3)).astype(BF16)
        yk_ref[6 * E + 16:8 * E, cols] = jnp.zeros((2 * E - 16, CB), BF16)
        return 0

    lax.fori_loop(0, HZ, prep_y, 0)

    lane = lax.broadcasted_iota(jnp.int32, (L, L), 1)
    left = lane < E

    def prep_x(h):
        def body(i, _):
            rows = ds(h * S + i * L, L)
            x = xs_ref[h, :, ds(i * L, L)] * (2.0 * BETA / E)
            x1, x2, x3 = (v.astype(F32) for v in split3(jnp.concatenate([x, x], 0).T))
            xk_ref[rows, 0:128] = x1.astype(BF16)
            xk_ref[rows, 128:256] = jnp.where(left, x2, x1).astype(BF16)
            xk_ref[rows, 256:384] = jnp.where(left, x2, x3).astype(BF16)
            xk_ref[rows, 384:512] = jnp.where(lane < 3, 1.0, 0.0).astype(BF16)
            mx_ref[rows, :] = jnp.full((L, L), -3e38, F32)
            sm_ref[rows, :] = jnp.zeros((L, L), F32)
            return 0

        lax.fori_loop(0, SR, body, 0)

    W2 = T2 // 2

    def scores(h, b):
        yk = yk_ref[:, b * W2:(b + 1) * W2]
        for i in range(S // RS):
            rows = ds(h * S + i * RS, RS)
            s = jnp.dot(xk_ref[rows, :], yk, preferred_element_type=F32)
            p_ref[rows, b * W2:(b + 1) * W2] = s
            old = mx_ref[rows, :]
            m = old
            for t in range(W2 // L):
                m = jnp.maximum(m, s[:, t * L:(t + 1) * L])
            acc = sm_ref[rows, :] * jnp.exp2(old - m)
            for t in range(W2 // L):
                acc = acc + jnp.exp2(s[:, t * L:(t + 1) * L] - m)
            mx_ref[rows, :] = m
            sm_ref[rows, :] = acc

    xs_ref[me_c] = x_ref[...]
    las_ref[me_c] = la_ref[...]
    prep_x(me_c)
    scores(me_c, 0)
    pl.semaphore_wait(barrier, greeted)
    base = sends.reserve(2)
    swap = [
        sends.copy(x_ref, xs_ref.at[me_c], base, base, partner),
        sends.copy(la_ref, las_ref.at[me_c], base + 1, base + 1, partner),
    ]
    for copy in swap:
        copy.start()
    sends.live += swap
    scores(me_c, 1)
    arrived(swap)
    prep_x(other)
    scores(other, 0)
    scores(other, 1)

    for i in range(NR):
        rows = slice(i * L, (i + 1) * L)
        m = mx_ref[rows, :].T
        top = jnp.max(m, 0, keepdims=True)
        tmp_ref[0, i:i + 1, :] = top
        tmp_ref[1, i:i + 1, :] = jnp.sum(sm_ref[rows, :].T * jnp.exp2(m - top), 0, keepdims=True)
    fm_ref[me_f] = tmp_ref[0] + jnp.log2(tmp_ref[1])
    f1 = exchange(lambda peer: fm_ref.at[me_f], fm_ref.at[me_f], me_f, 2 * NY, dev_f)

    la = jnp.concatenate([las_ref[0], las_ref[1]], 0)
    la2 = LOG2E * la

    def spread(a):
        for i in range(NR):
            vb_ref[i * L:(i + 1) * L, :] = jnp.broadcast_to(a[i:i + 1, :], (L, L)).T

    arrived(f1)
    lse = lse2(fm_ref, 2 * NY)
    spread(la2 - lse)

    def columns(b, _):
        cols = ds(b * CB, CB)

        def step(i, carry):
            old, acc = carry
            rows = ds(i * RC, RC)
            v = vb_ref[rows, :]
            t = (p_ref[rows, cols] + jnp.concatenate([v] * NX, 1)).reshape(RC // 8, 8, CB)
            m = jnp.maximum(old, jnp.max(t, 0))
            e = jnp.exp2(t - m)
            p_ref[rows, cols] = e.reshape(RC, CB)
            cm_ref[i, :, cols] = m
            return m, acc * jnp.exp2(old - m) + jnp.sum(e, 0)

        m, acc = lax.fori_loop(
            0, S2 // RC, step, (jnp.full((8, CB), -3e38, F32), jnp.zeros((8, CB), F32))
        )
        top = jnp.max(m, 0, keepdims=True)
        total = jnp.sum(acc * jnp.exp2(m - top), 0, keepdims=True)
        mf_ref[:, cols] = top
        for t in range(NX):
            tmp_ref[0, pl.ds(b * NX + t, 1), :] = top[:, t * L:(t + 1) * L]
            tmp_ref[1, pl.ds(b * NX + t, 1), :] = total[:, t * L:(t + 1) * L]
        return 0

    lax.fori_loop(0, HZ, columns, 0)

    m_col = tmp_ref[0, 0:NT]
    gx_ref[me_x] = m_col + jnp.log2(tmp_ref[1, 0:NT])
    gX = exchange(lambda peer: gx_ref.at[me_x], gx_ref.at[me_x], me_x, NX, dev_x)

    def settle(first, last):
        def body(i, _):
            rows = ds(i * RC, RC)
            for t in range(T2 // CB):
                lanes = slice(t * CB, (t + 1) * CB)
                fix = jnp.exp2(cm_ref[i, :, lanes] - mf_ref[:, lanes])
                e = (p_ref[rows, lanes].reshape(RC // 8, 8, CB) * fix).reshape(RC, CB)
                p_ref[rows, lanes] = e
                hi = e.astype(BF16)
                hi_ref[rows, lanes] = hi
                lo_ref[rows, lanes] = (e - hi.astype(F32)).astype(BF16)
            return 0

        lax.fori_loop(first, last, body, 0)

    steps = S2 // RC
    settle(0, steps // 2)
    arrived(gX)
    gz_ref[me_z] = lse2(gx_ref, NX)
    gZ = exchange(lambda peer: gz_ref.at[me_z], gz_ref.at[me_z], me_z, NZ, dev_z)
    settle(steps // 2, steps)
    arrived(gZ)
    g_lse = lse2(gz_ref, NZ)
    k = jnp.exp2(m_col - g_lse)
    k_ref[...] = k
    b_mine = lb_ref[ds(me_c * NT, NT), :]
    w_ref[...] = k * jnp.exp(b_mine)

    def row_dots(i, _):
        rows = ds(i * 64, 64)
        acc = jnp.zeros((64, L), F32)
        for t in range(NT):
            acc += p_ref[rows, t * L:(t + 1) * L] * w_ref[t:t + 1, :]
        sm_ref[rows, :] = acc
        return 0

    lax.fori_loop(0, S2 // 64, row_dots, 0)
    for i in range(NR):
        fr_ref[me_f, i:i + 1, :] = jnp.sum(sm_ref[i * L:(i + 1) * L, :].T, 0, keepdims=True)
    f2 = exchange(lambda peer: fr_ref.at[me_f], fr_ref.at[me_f], me_f, 2 * NY, dev_f)
    arrived(f2)
    total = add_up(fr_ref, 2 * NY)
    scale = jnp.exp(la) / total
    a_ref[...] = scale
    spread(scale)

    def column_dots(b, _):
        cols = ds(b * CB, CB)

        def step(i, acc):
            rows = ds(i * RS, RS)
            v = jnp.concatenate([vb_ref[rows, :]] * NX, 1)
            return acc + jnp.sum((p_ref[rows, cols] * v).reshape(RS // 8, 8, CB), 0)

        acc = lax.fori_loop(0, S2 // RS, step, jnp.zeros((8, CB), F32))
        acc = jnp.sum(acc, 0, keepdims=True)
        for t in range(NX):
            tmp_ref[0, pl.ds(b * NX + t, 1), :] = acc[:, t * L:(t + 1) * L]
        return 0

    lax.fori_loop(0, HZ, column_dots, 0)
    cx_ref[me_x] = tmp_ref[0, 0:NT] * k_ref[...]
    cX = exchange(lambda peer: cx_ref.at[me_x], cx_ref.at[me_x], me_x, NX, dev_x)

    mine = lambda v: jnp.where(me_c == 0, v[0:SR], v[SR:NR])
    potential = (jnp.log2(total) - la2 + lse) / BETA
    for i in range(SR):
        x = x_ref[:, i * L:(i + 1) * L]
        tmp_ref[1, i:i + 1, :] = jnp.sum(x * x, 0, keepdims=True) / E
    f_out[...] = tmp_ref[1, 0:SR] - mine(potential)

    for h in range(2):
        for i in range(SR):
            n = h * SR + i
            parts = split3(xs_ref[h, :, i * L:(i + 1) * L] * scale[n:n + 1, :])
            for j, part in enumerate(parts):
                xa_ref[j * E:(j + 1) * E, n * L:(n + 1) * L] = part

    def pulled(first, last):
        def body(b, _):
            cols = ds(b * CB, CB)
            out = jnp.dot(xa_ref[...], hi_ref[:, cols], preferred_element_type=F32)
            low = jnp.dot(xa_ref[0:2 * E, :], lo_ref[:, cols], preferred_element_type=F32)
            out = out[0:E] + out[E:2 * E] + out[2 * E:3 * E] + low[0:E] + low[E:2 * E]
            for t in range(NX):
                u_ref[t, b] = out[:, t * L:(t + 1) * L] * k_ref[pl.ds(b * NX + t, 1), :]
            return 0

        lax.fori_loop(first, last, body, 0)

    pulled(0, HZ // 2)
    arrived(cX)
    cz_ref[me_z] = add_up(cx_ref, NX)
    cZ = exchange(lambda peer: cz_ref.at[me_z], cz_ref.at[me_z], me_z, NZ, dev_z)
    pulled(HZ // 2, HZ)
    uX = exchange(lambda peer: u_ref.at[peer], r1_ref.at[me_x], me_x, NX, dev_x)
    arrived(cZ)
    d = add_up(cz_ref, NZ)
    d_ref[...] = d
    tmp_ref[0, 0:NT] = w_ref[...] / d

    def prep_b(b, _):
        cols = ds(b * CB, CB)
        right = jnp.concatenate([tmp_ref[0, pl.ds(b * NX + t, 1), :] for t in range(NX)], 1)
        for j, part in enumerate(split3(y_ref[:, ds(me_c * T2 + b * CB, CB)] * right)):
            yb_ref[j * E:(j + 1) * E, cols] = part
        b1, b2, b3 = split3(right)
        row = lax.broadcasted_iota(jnp.int32, (E, CB), 0)
        pick = lambda n, v: jnp.where(row == n, jnp.broadcast_to(v.astype(F32), (E, CB)), 0.0)
        yb_ref[3 * E:4 * E, cols] = (pick(0, b1) + pick(1, b2) + pick(2, b3)).astype(BF16)
        return 0

    lax.fori_loop(0, HZ, prep_b, 0)

    gs_ref[me_c] = (LOG2E * b_mine - g_lse - jnp.log2(d)) / BETA
    gC = exchange(lambda peer: gs_ref.at[me_c], gs_ref.at[me_c], me_c, 2, lambda j: {"src": chip + j})

    core_base = sends.reserve(NH)
    tgt_base = sends.reserve(NY)

    def core_copy(q):
        return sends.copy(so_ref.at[q], sc_ref.at[q], core_base + q, core_base + q, partner)

    def tgt_copy(owner, sender):
        return sends.copy(sy_ref.at[owner], sr_ref.at[sender], tgt_base + owner, tgt_base + sender, dev_y(owner))

    def moved(r, _):
        own = r >= NH
        h = jnp.where(own, me_c, other)
        q = jnp.where(own, lax.rem(r - NH + me_y // 2 + 1 + NH, NH), r)
        rows = ds(h * S + q * (2 * RB), 2 * RB)
        nt = (((1,), (1,)), ((), ()))
        out = lax.dot_general(hi_ref[rows, :], yb_ref[...], nt, preferred_element_type=F32)
        out = out + lax.dot_general(lo_ref[rows, :], yb_ref[...], nt, preferred_element_type=F32)
        out = out.T
        mass = out[3 * E:3 * E + 1] + out[3 * E + 1:3 * E + 2] + out[3 * E + 2:3 * E + 3]
        term = xs_ref[h, :, ds(q * (2 * RB), 2 * RB)] * mass - (out[0:E] + out[E:2 * E] + out[2 * E:3 * E])
        first = h * SR + q * (2 * RB // L)
        term = term * jnp.concatenate([a_ref[pl.ds(first + t, 1), :] for t in range(2 * RB // L)], 1)

        @pl.when(r < NH)
        def _():
            so_ref[q] = term
            core_copy(q).start()

        @pl.when(r >= NH)
        def _():
            core_copy(q).wait_recv()
            both = term + sc_ref[q]
            for e in range(2):
                owner = 2 * q + e
                part = both[:, e * RB:(e + 1) * RB]

                @pl.when(owner == me_y)
                def _():
                    sr_ref[me_y] = part

                @pl.when(owner != me_y)
                def _():
                    sy_ref[owner] = part
                    tgt_copy(owner, me_y).start()

        return 0

    lax.fori_loop(0, 2 * NH, moved, 0)

    arrived(uX)
    for j in range(HZ):
        total = u_ref[me_x, j]
        for r in range(1, NX):
            total = total + r1_ref[lax.rem(me_x + r, NX), j]
        t2_ref[j] = total
    z_base = sends.reserve(NZ)
    first_z = me_c * HZ
    holds = me_z // HZ == me_c

    def z_copy(j, sender):
        return sends.copy(t2_ref.at[j], r2_ref.at[sender], z_base + j, z_base + sender, dev_z(first_z + j))

    for j in range(HZ):
        @pl.when(first_z + j != me_z)
        def _():
            z_copy(j, me_z).start()

    for j in range(NY):
        @pl.when(j != me_y)
        def _():
            tgt_copy(me_y, j).wait_recv()

    sgb_ref[me_y] = add_up(sr_ref, NY)
    sY = exchange(lambda peer: sgb_ref.at[me_y], sgb_ref.at[me_y], me_y, NY, dev_y)

    tile_base = sends.reserve(1)
    tile_copy = sends.copy(tile_ref, tile_ref, tile_base, tile_base, partner)

    @pl.when(holds)
    def _():
        for j in range(NZ):
            @pl.when(j != me_z)
            def _():
                z_copy(0, j).wait_recv()

        total = t2_ref[me_z - first_z]
        for r in range(1, NZ):
            total = total + r2_ref[lax.rem(me_z + r, NZ)]
        here = (me_z - first_z) * NX + me_x
        b = jnp.exp(lb_ref[pl.ds(me_z * NX + me_x, 1), :])
        y = y_ref[:, ds((me_z * NX + me_x) * L, L)]
        tile_ref[...] = b * (y - total / d_ref[pl.ds(here, 1), :])
        tile_copy.start()

    @pl.when(jnp.logical_not(holds))
    def _():
        tile_copy.wait_recv()

    tile = tile_ref[...]
    tg_out[...] = jnp.where(me_c == 0, tile[:, 0:E], tile[:, E:2 * E])

    arrived(gC)
    g_out[0:NT] = gs_ref[0]
    g_out[NT:2 * NT] = gs_ref[1]

    arrived(sY)
    for j in range(NY):
        sg_out[:, j * RB:(j + 1) * RB] = sgb_ref[j]

    for copy in sends.live:
        copy.wait_send()
    for q in range(NH):
        core_copy(q).wait_send()
    for j in range(NY):
        @pl.when(j != me_y)
        def _():
            tgt_copy(j, me_y).wait_send()
    for j in range(HZ):
        @pl.when(first_z + j != me_z)
        def _():
            z_copy(j, me_z).wait_send()

    @pl.when(holds)
    def _():
        tile_copy.wait_send()


def local(dims, x, y, la, lb):
    NX, NZ, NY = dims
    E, S = x.shape
    T = y.shape[1]
    S2, T2 = 2 * S, T // 2
    HZ, NH, RB = NZ // 2, NY // 2, S // NY
    NT, NR, SR = T2 // L, S2 // L, S // L
    n_sems = 2 + 2 * (2 * NY - 1) + 3 * (NX - 1) + 2 * (NZ - 1) + 1 + NH + NY + NZ + (NY - 1) + 1
    big = max(NT, NR)
    vmem = lambda shape, dtype=F32: pltpu.VMEM(shape, dtype)
    f, g, sg, tg = pl.pallas_call(
        functools.partial(kernel, dims),
        out_shape=(
            jax.ShapeDtypeStruct((SR, L), F32),
            jax.ShapeDtypeStruct((2 * NT, L), F32),
            jax.ShapeDtypeStruct((E, S), F32),
            jax.ShapeDtypeStruct((E, 64), F32),
        ),
        in_specs=[pl.BlockSpec(memory_space=pltpu.VMEM)] * 4,
        out_specs=[pl.BlockSpec(memory_space=pltpu.VMEM)] * 4,
        scratch_shapes=[
            vmem((S2, T2)), vmem((S2, T2), BF16), vmem((S2, T2), BF16),
            vmem((S2, 8 * E), BF16), vmem((8 * E, T2), BF16),
            vmem((S2, L)), vmem((S2, L)), vmem((S2, L)),
            vmem((S2 // RC, 8, T2)), vmem((1, T2)),
            vmem((2, E, S)), vmem((2, SR, L)), vmem((2, big, L)),
            vmem((2 * NY, NR, L)), vmem((2 * NY, NR, L)),
            vmem((NX, NT, L)), vmem((NX, NT, L)), vmem((NZ, NT, L)), vmem((NT, L)), vmem((NT, L)),
            vmem((NR, L)), vmem((3 * E, S2), BF16), vmem((4 * E, T2), BF16),
            vmem((NX, NT, L)), vmem((NZ, NT, L)), vmem((NT, L)), vmem((2, NT, L)),
            vmem((NX, HZ, E, L)), vmem((NX, HZ, E, L)), vmem((HZ, E, L)), vmem((NZ, E, L)), vmem((E, L)),
            vmem((NH, E, 2 * RB)), vmem((NH, E, 2 * RB)),
            vmem((NY, E, RB)), vmem((NY, E, RB)), vmem((NY, E, RB)),
            pltpu.SemaphoreType.DMA((n_sems,)), pltpu.SemaphoreType.DMA((n_sems,)),
        ],
        compiler_params=pltpu.CompilerParams(
            collective_id=0, has_side_effects=True, vmem_limit_bytes=58 * 1024 * 1024
        ),
        cost_estimate=pl.CostEstimate(
            flops=2 * S2 * T2 * (8 + 5 + 8) * E, bytes_accessed=8 * E * (S + T), transcendentals=2 * S2 * T2
        ),
        name="sinkhorn",
    )(x, y, la.reshape(SR, L), lb.reshape(2 * NT, L))
    return f.reshape(S), g.reshape(T), sg, tg[:, None, :]


def solution(mesh):
    n_src, n_tgt = mesh.shape["src"], mesh.shape["tgt"]
    n_x = int(round((n_src // 4) ** 0.5))
    dims = (n_x, n_src // (2 * n_x), n_tgt)
    placed = (P(None, "src"), P(None, "tgt"), P("src"), P("tgt"))
    return jax.shard_map(
        functools.partial(local, dims),
        mesh=mesh,
        in_specs=placed,
        out_specs=(P("src"), P("tgt"), P(None, "src"), P(None, "tgt", "src")),
        check_vma=False,
    )
```

time: 1300 us -> 70.8 us (0.05); the launches traced: 1290 us -> 70.6 us
  blocking collectives: 1020 us -> 0 us
  waiting for transfers between devices: 115 us -> 0 us
  other arithmetic: 70.4 us -> 0 us
  Pallas kernels: 0 us -> 65.8 us
  matrix products: 52.9 us -> 0 us
  between operations: 15.8 us -> 0.65 us
    pmax x4 -> x0, blocking collectives: 516 us -> none  [the longest x2 499 us: column_lse(): top = lax.pmax(jnp.max(scores, 0), 'src')]
    psum x4 -> x0, blocking collectives: 505 us -> none  [the longest x2 493 us: column_lse(): total = lax.psum(jnp.sum(jnp.exp(scores - top[None, :]), 0), 'src')]
    unnamed x3 -> x0, waiting for transfers between devices: 115 us -> none
    pallas_call x0 -> x1, Pallas kernels: none -> 65.8 us  [local(): pl.pallas_call(functools.partial(kernel, dims), out_shape=(jax.ShapeDtype...]
    dot_general x3 -> x0, matrix products: 52.9 us -> none  [the longest x1 21.3 us: pair_cost(): lax.dot_general(points_a, points_b, (((0,), (0,)), ((), ())), precision=l...]
    reduce_sum x7 -> x0, other arithmetic: 44.1 us -> none  [the longest x2 16.2 us: row_lse(): total = lax.psum(jnp.sum(jnp.exp(scores - top[:, None]), 1), 'tgt')]
    reduce_max x3 -> x0, other arithmetic: 26.3 us -> none  [the longest x2 18.3 us: column_lse(): top = lax.pmax(jnp.max(scores, 0), 'src')]
  transfers between devices with their start and end apart: 2 -> 0, of which waited for: 1 -> 0; matrix products, arithmetic and copies ran while one was open for 2% -> 0% of each run, Pallas kernels for 0% -> 0%
where the time goes in v2:
time: 70.8 us; the launch traced here: 70.6 us
  Pallas kernels  65.8 us (93%)
  local copies, waits for them, and re-layouts  4.18 us (6%)
    pallas_call x1, Pallas kernels, local(): pl.pallas_call(functools.partial(kernel, dims), out_shape=(jax.ShapeDtype...  65.8 us
    unnamed x8, local copies, waits for them, and re-layouts  4.18 us

profile of v2, /device:TPU:1, one launch (start us, length us, event | category | flops | bytes accessed | tf_op | source)
XLA Modules:
  0.0 70.6 jit_solution(457307642919820740)
XLA Ops:
  0.6 65.8 %sinkhorn.1 = (f32[8,128]{1,0:T(8,128)}, f32[32,128]{1,0:T(8,128)}, f32[64,1024]{1,0:T(8,128)}, f32[64,64]{1,0:T(8,128)}) custom-call(f32[64,1024]{1,0:T(8,128)} %x_ref.1, f32[64,4096]{1,0:T(8,128)} %y_ref.1, f32[8,128]{1,0:T(8,128)} %bitcast.11, f32[32,128]{1,0:T(8,128)} %bitcast.10), custom_call_target="tpu_custom_call" | custom-call | flops 11274289152 | bytes 2621440 | tf_op jit(solution)/shard_map/sinkhorn/pallas_call | solution.py:509
  66.4 0.0 copy-start.1
  66.4 1.3 %copy.13 = f32[1024]{0:T(1024)} copy(f32[1024]{0:T(1024)} %bitcast.9) | data formatting | bytes 8192
  67.7 0.0 copy-done.1
  67.7 0.6 copy.14
  68.3 0.0 copy-start
  68.3 1.7 %copy.15 = f32[64,1024]{1,0:T(8,128)} copy(f32[64,1024]{1,0:T(8,128)} %get-tuple-element.22) | data formatting | bytes 524288
  70.0 0.0 copy-done
  70.0 0.6 copy.16
Async XLA Ops:
  66.4 1.3 %copy-start.1 = (f32[32,128]{1,0:T(8,128)S(1)}, f32[32,128]{1,0:T(8,128)}, u32[]{:S(2)}) copy-start(f32[32,128]{1,0:T(8,128)} %get-tuple-element.9) | copy-start | bytes 49156
  68.3 1.7 %copy-start = (f32[64,64]{1,0:T(8,128)S(1)}, f32[64,64]{1,0:T(8,128)}, u32[]{:S(2)}) copy-start(f32[64,64]{1,0:T(8,128)} %get-tuple-element.11) | copy-start | bytes 49156

commit v3 on v2

--- a/solution.py
+++ b/solution.py
@@ -85,22 +85,21 @@
         copy.wait_recv()
 
 
-def kernel(dims, x_ref, y_ref, la_ref, lb_ref,
+def kernel(dims, x_ref, y_hbm, la_ref, lb_ref,
            f_out, g_out, sg_out, tg_out,
            p_ref, hi_ref, lo_ref, xk_ref, yk_ref, mx_ref, sm_ref, vb_ref, cm_ref, mf_ref,
-           xs_ref, las_ref, tmp_ref, fm_ref, fr_ref, gm_ref, gx_ref, gz_ref, k_ref, w_ref,
+           xs_ref, las_ref, tmp_ref, run_ref, fc_ref, fm_ref, frc_ref, fr_ref, gm_ref, gx_ref, gz_ref, k_ref, w_ref,
            a_ref, xa_ref, yb_ref, cx_ref, cz_ref, d_ref, gs_ref,
            u_ref, r1_ref, t2_ref, r2_ref, tile_ref, so_ref, sc_ref, sy_ref, sr_ref, sgb_ref,
-           send_sems, recv_sems):
+           y_ref, send_sems, recv_sems, y_sems):
     NX, NZ, NY = dims
     NQ = 2 * NX
     E, S = x_ref.shape
-    T = y_ref.shape[1]
+    T = y_hbm.shape[1]
     T2, S2 = T // 2, 2 * S
     HZ = NZ // 2
     CB = NX * L
     RB = S // NY
-    NH = NY // 2
     NT, NR, SR = T2 // L, S2 // L, S // L
 
     src = lax.axis_index("src")
@@ -110,10 +109,9 @@
     me_x = me_q // 2
     me_c = lax.rem(me_q, 2)
     other = 1 - me_c
-    me_f = me_y * 2 + me_c
     chip = src - me_c
 
-    dev_f = lambda j: {"src": chip + lax.rem(j, 2), "tgt": j // 2}
+    dev_c = lambda j: {"src": chip + j}
     dev_y = lambda j: {"tgt": j}
     dev_z = lambda j: {"src": j * NQ + me_q}
     dev_x = lambda j: {"src": me_z * NQ + j * 2 + me_c}
@@ -122,16 +120,25 @@
     sends = Sends(send_sems, recv_sems)
     exchange = sends.exchange
 
+    loads = [
+        pltpu.make_async_copy(
+            y_hbm.at[:, ds(me_c * T2 + b * CB, CB)], y_ref.at[:, b * CB:(b + 1) * CB], y_sems.at[b]
+        )
+        for b in range(HZ)
+    ]
+    for load in loads:
+        load.start()
+
     barrier = pltpu.get_barrier_semaphore()
     greeted = 0
-    for me, n, device in ((me_f, 2 * NY, dev_f), (me_x, NX, dev_x), (me_z, NZ, dev_z)):
+    for me, n, device in ((me_c, 2, dev_c), (me_y, NY, dev_y), (me_x, NX, dev_x), (me_z, NZ, dev_z)):
         for r in range(1, n):
             pl.semaphore_signal(barrier, inc=1, device_id=device(lax.rem(me + r, n)), device_id_type=MESH)
             greeted += 1
 
     def prep_y(b, _):
         cols = ds(b * CB, CB)
-        y = y_ref[:, ds(me_c * T2 + b * CB, CB)]
+        y = y_ref[:, cols]
         y1, y2, y3 = split3(y)
         for n, part in enumerate((y1, y2, y1, y3, y2, y1)):
             yk_ref[n * E:(n + 1) * E, cols] = part
@@ -144,7 +151,6 @@
         yk_ref[6 * E + 16:8 * E, cols] = jnp.zeros((2 * E - 16, CB), BF16)
         return 0
 
-    lax.fori_loop(0, HZ, prep_y, 0)
 
     lane = lax.broadcasted_iota(jnp.int32, (L, L), 1)
     left = lane < E
@@ -185,6 +191,9 @@
     xs_ref[me_c] = x_ref[...]
     las_ref[me_c] = la_ref[...]
     prep_x(me_c)
+    for load in loads:
+        load.wait()
+    lax.fori_loop(0, HZ, prep_y, 0)
     scores(me_c, 0)
     pl.semaphore_wait(barrier, greeted)
     base = sends.reserve(2)
@@ -207,8 +216,8 @@
         top = jnp.max(m, 0, keepdims=True)
         tmp_ref[0, i:i + 1, :] = top
         tmp_ref[1, i:i + 1, :] = jnp.sum(sm_ref[rows, :].T * jnp.exp2(m - top), 0, keepdims=True)
-    fm_ref[me_f] = tmp_ref[0] + jnp.log2(tmp_ref[1])
-    f1 = exchange(lambda peer: fm_ref.at[me_f], fm_ref.at[me_f], me_f, 2 * NY, dev_f)
+    fc_ref[me_c] = tmp_ref[0] + jnp.log2(tmp_ref[1])
+    f1c = exchange(lambda peer: fc_ref.at[me_c], fc_ref.at[me_c], me_c, 2, dev_c)
 
     la = jnp.concatenate([las_ref[0], las_ref[1]], 0)
     la2 = LOG2E * la
@@ -217,36 +226,38 @@
         for i in range(NR):
             vb_ref[i * L:(i + 1) * L, :] = jnp.broadcast_to(a[i:i + 1, :], (L, L)).T
 
+    arrived(f1c)
+    fm_ref[me_y] = lse2(fc_ref, 2)
+    f1 = exchange(lambda peer: fm_ref.at[me_y], fm_ref.at[me_y], me_y, NY, dev_y)
+    run_ref[0] = jnp.full((8, T2), -3e38, F32)
+    run_ref[1] = jnp.zeros((8, T2), F32)
     arrived(f1)
-    lse = lse2(fm_ref, 2 * NY)
+    lse = lse2(fm_ref, NY)
     spread(la2 - lse)
 
-    def columns(b, _):
-        cols = ds(b * CB, CB)
-
-        def step(i, carry):
-            old, acc = carry
-            rows = ds(i * RC, RC)
-            v = vb_ref[rows, :]
-            t = (p_ref[rows, cols] + jnp.concatenate([v] * NX, 1)).reshape(RC // 8, 8, CB)
+    def columns(i, _):
+        rows = ds(i * RC, RC)
+        v = jnp.concatenate([vb_ref[rows, :]] * NX, 1)
+        for b in range(HZ):
+            cols = slice(b * CB, (b + 1) * CB)
+            t = (p_ref[rows, cols] + v).reshape(RC // 8, 8, CB)
+            old = run_ref[0, :, cols]
             m = jnp.maximum(old, jnp.max(t, 0))
             e = jnp.exp2(t - m)
             p_ref[rows, cols] = e.reshape(RC, CB)
             cm_ref[i, :, cols] = m
-            return m, acc * jnp.exp2(old - m) + jnp.sum(e, 0)
-
-        m, acc = lax.fori_loop(
-            0, S2 // RC, step, (jnp.full((8, CB), -3e38, F32), jnp.zeros((8, CB), F32))
-        )
+            run_ref[0, :, cols] = m
+            run_ref[1, :, cols] = run_ref[1, :, cols] * jnp.exp2(old - m) + jnp.sum(e, 0)
+        return 0
+
+    lax.fori_loop(0, S2 // RC, columns, 0)
+    for t in range(NT):
+        cols = slice(t * L, (t + 1) * L)
+        m = run_ref[0, :, cols]
         top = jnp.max(m, 0, keepdims=True)
-        total = jnp.sum(acc * jnp.exp2(m - top), 0, keepdims=True)
         mf_ref[:, cols] = top
-        for t in range(NX):
-            tmp_ref[0, pl.ds(b * NX + t, 1), :] = top[:, t * L:(t + 1) * L]
-            tmp_ref[1, pl.ds(b * NX + t, 1), :] = total[:, t * L:(t + 1) * L]
-        return 0
-
-    lax.fori_loop(0, HZ, columns, 0)
+        tmp_ref[0, t:t + 1, :] = top
+        tmp_ref[1, t:t + 1, :] = jnp.sum(run_ref[1, :, cols] * jnp.exp2(m - top), 0, keepdims=True)
 
     m_col = tmp_ref[0, 0:NT]
     gx_ref[me_x] = m_col + jnp.log2(tmp_ref[1, 0:NT])
@@ -281,19 +292,22 @@
     w_ref[...] = k * jnp.exp(b_mine)
 
     def row_dots(i, _):
-        rows = ds(i * 64, 64)
-        acc = jnp.zeros((64, L), F32)
+        rows = ds(i * RS, RS)
+        acc = jnp.zeros((RS, L), F32)
         for t in range(NT):
             acc += p_ref[rows, t * L:(t + 1) * L] * w_ref[t:t + 1, :]
         sm_ref[rows, :] = acc
         return 0
 
-    lax.fori_loop(0, S2 // 64, row_dots, 0)
+    lax.fori_loop(0, S2 // RS, row_dots, 0)
     for i in range(NR):
-        fr_ref[me_f, i:i + 1, :] = jnp.sum(sm_ref[i * L:(i + 1) * L, :].T, 0, keepdims=True)
-    f2 = exchange(lambda peer: fr_ref.at[me_f], fr_ref.at[me_f], me_f, 2 * NY, dev_f)
+        frc_ref[me_c, i:i + 1, :] = jnp.sum(sm_ref[i * L:(i + 1) * L, :].T, 0, keepdims=True)
+    f2c = exchange(lambda peer: frc_ref.at[me_c], frc_ref.at[me_c], me_c, 2, dev_c)
+    arrived(f2c)
+    fr_ref[me_y] = add_up(frc_ref, 2)
+    f2 = exchange(lambda peer: fr_ref.at[me_y], fr_ref.at[me_y], me_y, NY, dev_y)
     arrived(f2)
-    total = add_up(fr_ref, 2 * NY)
+    total = add_up(fr_ref, NY)
     scale = jnp.exp(la) / total
     a_ref[...] = scale
     spread(scale)
@@ -306,7 +320,7 @@
             v = jnp.concatenate([vb_ref[rows, :]] * NX, 1)
             return acc + jnp.sum((p_ref[rows, cols] * v).reshape(RS // 8, 8, CB), 0)
 
-        acc = lax.fori_loop(0, S2 // RS, step, jnp.zeros((8, CB), F32))
+        acc = lax.fori_loop(0, S2 // RS, step, jnp.zeros((8, CB), F32), unroll=2)
         acc = jnp.sum(acc, 0, keepdims=True)
         for t in range(NX):
             tmp_ref[0, pl.ds(b * NX + t, 1), :] = acc[:, t * L:(t + 1) * L]
@@ -346,8 +360,10 @@
     arrived(cX)
     cz_ref[me_z] = add_up(cx_ref, NX)
     cZ = exchange(lambda peer: cz_ref.at[me_z], cz_ref.at[me_z], me_z, NZ, dev_z)
-    pulled(HZ // 2, HZ)
-    uX = exchange(lambda peer: u_ref.at[peer], r1_ref.at[me_x], me_x, NX, dev_x)
+    H2 = HZ // 2
+    uX = exchange(lambda peer: u_ref.at[peer, 0:H2], r1_ref.at[me_x, 0:H2], me_x, NX, dev_x)
+    pulled(H2, HZ)
+    uX += exchange(lambda peer: u_ref.at[peer, H2:HZ], r1_ref.at[me_x, H2:HZ], me_x, NX, dev_x)
     arrived(cZ)
     d = add_up(cz_ref, NZ)
     d_ref[...] = d
@@ -356,7 +372,7 @@
     def prep_b(b, _):
         cols = ds(b * CB, CB)
         right = jnp.concatenate([tmp_ref[0, pl.ds(b * NX + t, 1), :] for t in range(NX)], 1)
-        for j, part in enumerate(split3(y_ref[:, ds(me_c * T2 + b * CB, CB)] * right)):
+        for j, part in enumerate(split3(y_ref[:, cols] * right)):
             yb_ref[j * E:(j + 1) * E, cols] = part
         b1, b2, b3 = split3(right)
         row = lax.broadcasted_iota(jnp.int32, (E, CB), 0)
@@ -367,56 +383,60 @@
     lax.fori_loop(0, HZ, prep_b, 0)
 
     gs_ref[me_c] = (LOG2E * b_mine - g_lse - jnp.log2(d)) / BETA
-    gC = exchange(lambda peer: gs_ref.at[me_c], gs_ref.at[me_c], me_c, 2, lambda j: {"src": chip + j})
-
-    core_base = sends.reserve(NH)
-    tgt_base = sends.reserve(NY)
-
-    def core_copy(q):
-        return sends.copy(so_ref.at[q], sc_ref.at[q], core_base + q, core_base + q, partner)
-
-    def tgt_copy(owner, sender):
-        return sends.copy(sy_ref.at[owner], sr_ref.at[sender], tgt_base + owner, tgt_base + sender, dev_y(owner))
-
-    def moved(r, _):
-        own = r >= NH
-        h = jnp.where(own, me_c, other)
-        q = jnp.where(own, lax.rem(r - NH + me_y // 2 + 1 + NH, NH), r)
-        rows = ds(h * S + q * (2 * RB), 2 * RB)
+    gC = exchange(lambda peer: gs_ref.at[me_c], gs_ref.at[me_c], me_c, 2, dev_c)
+
+    core_base = sends.reserve(2)
+    tgt_base = sends.reserve(2 * NY)
+    RH = RB // 2
+
+    def core_copy(n):
+        return sends.copy(so_ref.at[n], sc_ref.at[n], core_base + n, core_base + n, partner)
+
+    def tgt_copy(n, owner, sender):
+        base = tgt_base + n * NY
+        return sends.copy(sy_ref.at[n, owner], sr_ref.at[n, sender], base + owner, base + sender, dev_y(owner))
+
+    def moved(h, n):
+        starts = [h * S + j * RB + n * RH for j in range(NY)]
         nt = (((1,), (1,)), ((), ()))
-        out = lax.dot_general(hi_ref[rows, :], yb_ref[...], nt, preferred_element_type=F32)
-        out = out + lax.dot_general(lo_ref[rows, :], yb_ref[...], nt, preferred_element_type=F32)
+        block = lambda ref: jnp.concatenate([ref[ds(start, RH), :] for start in starts], 0)
+        out = lax.dot_general(block(hi_ref), yb_ref[...], nt, preferred_element_type=F32)
+        out = out + lax.dot_general(block(lo_ref), yb_ref[...], nt, preferred_element_type=F32)
         out = out.T
         mass = out[3 * E:3 * E + 1] + out[3 * E + 1:3 * E + 2] + out[3 * E + 2:3 * E + 3]
-        term = xs_ref[h, :, ds(q * (2 * RB), 2 * RB)] * mass - (out[0:E] + out[E:2 * E] + out[2 * E:3 * E])
-        first = h * SR + q * (2 * RB // L)
-        term = term * jnp.concatenate([a_ref[pl.ds(first + t, 1), :] for t in range(2 * RB // L)], 1)
-
-        @pl.when(r < NH)
-        def _():
-            so_ref[q] = term
-            core_copy(q).start()
-
-        @pl.when(r >= NH)
-        def _():
-            core_copy(q).wait_recv()
-            both = term + sc_ref[q]
-            for e in range(2):
-                owner = 2 * q + e
-                part = both[:, e * RB:(e + 1) * RB]
-
-                @pl.when(owner == me_y)
-                def _():
-                    sr_ref[me_y] = part
-
-                @pl.when(owner != me_y)
-                def _():
-                    sy_ref[owner] = part
-                    tgt_copy(owner, me_y).start()
-
+        out = out[0:E] + out[E:2 * E] + out[2 * E:3 * E]
+        terms = []
+        for j in range(NY):
+            here = slice(j * RH, (j + 1) * RH)
+            x = xs_ref[h, :, ds(j * RB + n * RH, RH)]
+            first = h * SR + (j * RB + n * RH) // L
+            a = jnp.concatenate([a_ref[pl.ds(first + t, 1), :] for t in range(RH // L)], 1)
+            terms.append((x * mass[:, here] - out[:, here]) * a)
+        return terms
+
+    def moved_other(n, _):
+        for j, term in enumerate(moved(other, n)):
+            so_ref[n, j] = term
+        core_copy(n).start()
         return 0
 
-    lax.fori_loop(0, 2 * NH, moved, 0)
+    def moved_own(n):
+        terms = moved(me_c, n)
+        core_copy(n).wait_recv()
+        for j, term in enumerate(terms):
+            term = term + sc_ref[n, j]
+
+            @pl.when(j == me_y)
+            def _():
+                sr_ref[n, me_y] = term
+
+            @pl.when(j != me_y)
+            def _():
+                sy_ref[n, j] = term
+                tgt_copy(n, j, me_y).start()
+
+    lax.fori_loop(0, 2, moved_other, 0)
+    moved_own(0)
 
     arrived(uX)
     for j in range(HZ):
@@ -436,13 +456,17 @@
         def _():
             z_copy(j, me_z).start()
 
-    for j in range(NY):
-        @pl.when(j != me_y)
-        def _():
-            tgt_copy(me_y, j).wait_recv()
-
-    sgb_ref[me_y] = add_up(sr_ref, NY)
-    sY = exchange(lambda peer: sgb_ref.at[me_y], sgb_ref.at[me_y], me_y, NY, dev_y)
+    moved_own(1)
+
+    sY = []
+    for n in range(2):
+        for j in range(NY):
+            @pl.when(j != me_y)
+            def _():
+                tgt_copy(n, me_y, j).wait_recv()
+
+        sgb_ref[n, me_y] = add_up(sr_ref.at[n], NY)
+        sY += exchange(lambda peer: sgb_ref.at[n, me_y], sgb_ref.at[n, me_y], me_y, NY, dev_y)
 
     tile_base = sends.reserve(1)
     tile_copy = sends.copy(tile_ref, tile_ref, tile_base, tile_base, partner)
@@ -459,7 +483,7 @@
             total = total + r2_ref[lax.rem(me_z + r, NZ)]
         here = (me_z - first_z) * NX + me_x
         b = jnp.exp(lb_ref[pl.ds(me_z * NX + me_x, 1), :])
-        y = y_ref[:, ds((me_z * NX + me_x) * L, L)]
+        y = y_ref[:, ds(here * L, L)]
         tile_ref[...] = b * (y - total / d_ref[pl.ds(here, 1), :])
         tile_copy.start()
 
@@ -468,24 +492,26 @@
         tile_copy.wait_recv()
 
     tile = tile_ref[...]
-    tg_out[...] = jnp.where(me_c == 0, tile[:, 0:E], tile[:, E:2 * E])
+    tg_out[:, 0, :] = jnp.where(me_c == 0, tile[:, 0:E], tile[:, E:2 * E])
 
     arrived(gC)
     g_out[0:NT] = gs_ref[0]
     g_out[NT:2 * NT] = gs_ref[1]
 
     arrived(sY)
-    for j in range(NY):
-        sg_out[:, j * RB:(j + 1) * RB] = sgb_ref[j]
+    for n in range(2):
+        for j in range(NY):
+            sg_out[:, j * RB + n * RH:j * RB + (n + 1) * RH] = sgb_ref[n, j]
 
     for copy in sends.live:
         copy.wait_send()
-    for q in range(NH):
-        core_copy(q).wait_send()
-    for j in range(NY):
-        @pl.when(j != me_y)
-        def _():
-            tgt_copy(j, me_y).wait_send()
+    for n in range(2):
+        core_copy(n).wait_send()
+        for j in range(NY):
+            @pl.when(j != me_y)
+            def _():
+                tgt_copy(n, j, me_y).wait_send()
+
     for j in range(HZ):
         @pl.when(first_z + j != me_z)
         def _():
@@ -494,6 +520,27 @@
     @pl.when(holds)
     def _():
         tile_copy.wait_send()
+
+
+def finish_kernel(*refs):
+    n = len(refs) // 2
+    copies = [pltpu.make_async_copy(refs[i], refs[n + i], refs[-1].at[i]) for i in range(n)]
+    for copy in copies:
+        copy.start()
+    for copy in copies:
+        copy.wait()
+
+
+def finish(*arrays):
+    return pl.pallas_call(
+        finish_kernel,
+        out_shape=tuple(jax.ShapeDtypeStruct(a.shape, a.dtype) for a in arrays),
+        in_specs=[pl.BlockSpec(memory_space=pl.ANY)] * len(arrays),
+        out_specs=[pl.BlockSpec(memory_space=pl.ANY)] * len(arrays),
+        scratch_shapes=[pltpu.SemaphoreType.DMA((len(arrays),))],
+        compiler_params=pltpu.CompilerParams(vmem_limit_bytes=58 * 1024 * 1024),
+        name="results",
+    )(*arrays)
 
 
 def local(dims, x, y, la, lb):
@@ -501,9 +548,9 @@
     E, S = x.shape
     T = y.shape[1]
     S2, T2 = 2 * S, T // 2
-    HZ, NH, RB = NZ // 2, NY // 2, S // NY
+    HZ, RB = NZ // 2, S // NY
     NT, NR, SR = T2 // L, S2 // L, S // L
-    n_sems = 2 + 2 * (2 * NY - 1) + 3 * (NX - 1) + 2 * (NZ - 1) + 1 + NH + NY + NZ + (NY - 1) + 1
+    n_sems = 2 + 2 * NY + 4 * (NX - 1) + 2 * (NZ - 1) + 1 + 2 + 2 * NY + NZ + 2 * (NY - 1) + 1
     big = max(NT, NR)
     vmem = lambda shape, dtype=F32: pltpu.VMEM(shape, dtype)
     f, g, sg, tg = pl.pallas_call(
@@ -512,9 +559,9 @@
             jax.ShapeDtypeStruct((SR, L), F32),
             jax.ShapeDtypeStruct((2 * NT, L), F32),
             jax.ShapeDtypeStruct((E, S), F32),
-            jax.ShapeDtypeStruct((E, 64), F32),
+            jax.ShapeDtypeStruct((E, 1, 64), F32),
         ),
-        in_specs=[pl.BlockSpec(memory_space=pltpu.VMEM)] * 4,
+        in_specs=[pl.BlockSpec(memory_space=pl.ANY if i == 1 else pltpu.VMEM) for i in range(4)],
         out_specs=[pl.BlockSpec(memory_space=pltpu.VMEM)] * 4,
         scratch_shapes=[
             vmem((S2, T2)), vmem((S2, T2), BF16), vmem((S2, T2), BF16),
@@ -522,14 +569,15 @@
             vmem((S2, L)), vmem((S2, L)), vmem((S2, L)),
             vmem((S2 // RC, 8, T2)), vmem((1, T2)),
             vmem((2, E, S)), vmem((2, SR, L)), vmem((2, big, L)),
-            vmem((2 * NY, NR, L)), vmem((2 * NY, NR, L)),
+            vmem((2, 8, T2)), vmem((2, NR, L)), vmem((NY, NR, L)), vmem((2, NR, L)), vmem((NY, NR, L)),
             vmem((NX, NT, L)), vmem((NX, NT, L)), vmem((NZ, NT, L)), vmem((NT, L)), vmem((NT, L)),
             vmem((NR, L)), vmem((3 * E, S2), BF16), vmem((4 * E, T2), BF16),
             vmem((NX, NT, L)), vmem((NZ, NT, L)), vmem((NT, L)), vmem((2, NT, L)),
             vmem((NX, HZ, E, L)), vmem((NX, HZ, E, L)), vmem((HZ, E, L)), vmem((NZ, E, L)), vmem((E, L)),
-            vmem((NH, E, 2 * RB)), vmem((NH, E, 2 * RB)),
-            vmem((NY, E, RB)), vmem((NY, E, RB)), vmem((NY, E, RB)),
-            pltpu.SemaphoreType.DMA((n_sems,)), pltpu.SemaphoreType.DMA((n_sems,)),
+            vmem((2, NY, E, RB // 2)), vmem((2, NY, E, RB // 2)),
+            vmem((2, NY, E, RB // 2)), vmem((2, NY, E, RB // 2)), vmem((2, NY, E, RB // 2)),
+            vmem((E, T2)),
+            pltpu.SemaphoreType.DMA((n_sems,)), pltpu.SemaphoreType.DMA((n_sems,)), pltpu.SemaphoreType.DMA((HZ,)),
         ],
         compiler_params=pltpu.CompilerParams(
             collective_id=0, has_side_effects=True, vmem_limit_bytes=58 * 1024 * 1024
@@ -539,7 +587,8 @@
         ),
         name="sinkhorn",
     )(x, y, la.reshape(SR, L), lb.reshape(2 * NT, L))
-    return f.reshape(S), g.reshape(T), sg, tg[:, None, :]
+    f, g, sg, tg = finish(f, g, sg, tg)
+    return f.reshape(S), g.reshape(T), sg, tg
 
 
 def solution(mesh):

time: 70.8 us -> 76 us (1.073)
  Pallas kernels: 65.8 us -> 75 us
  local copies, waits for them, and re-layouts: 4.18 us -> 0 us
    pallas_call x0 -> x1, Pallas kernels: none -> 10.7 us  [finish(): pl.pallas_call(finish_kernel, out_shape=tuple((jax.ShapeDtypeStruct(a.sha...]
    unnamed x8 -> x0, local copies, waits for them, and re-layouts: 4.18 us -> none
    pallas_call x1, Pallas kernels: 65.8 us -> 64.3 us  [local(): pl.pallas_call(functools.partial(kernel, dims), out_shape=(jax.ShapeDtype...]
where the time goes in v3:
time: 76 us; the launch traced here: 75.7 us
  Pallas kernels  75 us (99%)
    pallas_call x1, Pallas kernels, local(): pl.pallas_call(functools.partial(kernel, dims), out_shape=(jax.ShapeDtype...  64.3 us
    pallas_call x1, Pallas kernels, finish(): pl.pallas_call(finish_kernel, out_shape=tuple((jax.ShapeDtypeStruct(a.sha...  10.7 us

profile of v3, /device:TPU:1, one launch (start us, length us, event | category | flops | bytes accessed | tf_op | source)
XLA Modules:
  0.0 75.7 jit_solution(6636144567284874621)
XLA Ops:
  0.6 64.3 %sinkhorn.1 = (f32[8,128]{1,0:T(8,128)}, f32[32,128]{1,0:T(8,128)}, f32[64,1024]{1,0:T(8,128)}, f32[64,1,64]{2,1,0:T(1,128)}) custom-call(f32[64,1024]{1,0:T(8,128)} %x_ref.1, f32[64,4096]{1,0:T(8,128)} %y_hbm.1, f32[8,128]{1,0:T(8,128)} %bitcast.6, f32[32,128]{1,0:T(8,128)} %bitcast.4), custom_call_target="tpu_custom_call" | custom-call | flops 11274289152 | bytes 2621440 | tf_op jit(solution)/shard_map/sinkhorn/pallas_call | solution.py:556
  65.0 10.7 %results.1 = (f32[8,128]{1,0:T(8,128)}, f32[32,128]{1,0:T(8,128)}, f32[64,1024]{1,0:T(8,128)}, f32[64,1,64]{2,1,0:T(1,128)}) custom-call(f32[8,128]{1,0:T(8,128)} %get-tuple-element.12.refs_0_, f32[32,128]{1,0:T(8,128)} %get-tuple-element.13.refs_1_, f32[64,1024]{1,0:T(8,128)} %get-tuple-element.14.refs_2_, f32[64,1,64]{2,1,0:T(1,128)} %get-tuple-element.15.refs_3_), custom_call_target="tpu_custom_call" | custom-call | tf_op jit(solution)/shard_map/results/pallas_call | solution.py:535

commit v4 on v3

--- a/solution.py
+++ b/solution.py
@@ -392,51 +392,52 @@
     def core_copy(n):
         return sends.copy(so_ref.at[n], sc_ref.at[n], core_base + n, core_base + n, partner)
 
-    def tgt_copy(n, owner, sender):
-        base = tgt_base + n * NY
-        return sends.copy(sy_ref.at[n, owner], sr_ref.at[n, sender], base + owner, base + sender, dev_y(owner))
-
-    def moved(h, n):
-        starts = [h * S + j * RB + n * RH for j in range(NY)]
+    def tgt_copy(n, r):
+        sem = tgt_base + n * NY + r
+        return sends.copy(sy_ref.at[n, r], sr_ref.at[n, me_y], sem, sem, dev_y(lax.rem(me_y + r, NY)))
+
+    owners = [lax.rem(me_y + r, NY) for r in range(NY)]
+
+    def dots(h, n):
         nt = (((1,), (1,)), ((), ()))
-        block = lambda ref: jnp.concatenate([ref[ds(start, RH), :] for start in starts], 0)
+        block = lambda ref: jnp.concatenate([ref[ds(h * S + j * RB + n * RH, RH), :] for j in owners], 0)
         out = lax.dot_general(block(hi_ref), yb_ref[...], nt, preferred_element_type=F32)
-        out = out + lax.dot_general(block(lo_ref), yb_ref[...], nt, preferred_element_type=F32)
+        return out + lax.dot_general(block(lo_ref), yb_ref[...], nt, preferred_element_type=F32)
+
+    def terms(h, n, out):
         out = out.T
         mass = out[3 * E:3 * E + 1] + out[3 * E + 1:3 * E + 2] + out[3 * E + 2:3 * E + 3]
         out = out[0:E] + out[E:2 * E] + out[2 * E:3 * E]
-        terms = []
-        for j in range(NY):
-            here = slice(j * RH, (j + 1) * RH)
+        result = []
+        for r, j in enumerate(owners):
+            here = slice(r * RH, (r + 1) * RH)
             x = xs_ref[h, :, ds(j * RB + n * RH, RH)]
             first = h * SR + (j * RB + n * RH) // L
             a = jnp.concatenate([a_ref[pl.ds(first + t, 1), :] for t in range(RH // L)], 1)
-            terms.append((x * mass[:, here] - out[:, here]) * a)
-        return terms
-
-    def moved_other(n, _):
-        for j, term in enumerate(moved(other, n)):
-            so_ref[n, j] = term
+            result.append((x * mass[:, here] - out[:, here]) * a)
+        return result
+
+    def to_partner(n, out):
+        for r, term in enumerate(terms(other, n, out)):
+            so_ref[n, owners[r]] = term
         core_copy(n).start()
-        return 0
-
-    def moved_own(n):
-        terms = moved(me_c, n)
+
+    def to_owners(n, out):
         core_copy(n).wait_recv()
-        for j, term in enumerate(terms):
-            term = term + sc_ref[n, j]
-
-            @pl.when(j == me_y)
-            def _():
+        for r, term in enumerate(terms(me_c, n, out)):
+            term = term + sc_ref[n, owners[r]]
+            if r == 0:
                 sr_ref[n, me_y] = term
-
-            @pl.when(j != me_y)
-            def _():
-                sy_ref[n, j] = term
-                tgt_copy(n, j, me_y).start()
-
-    lax.fori_loop(0, 2, moved_other, 0)
-    moved_own(0)
+            else:
+                sy_ref[n, r] = term
+        for r in range(1, NY):
+            tgt_copy(n, r).start()
+
+    out0 = dots(other, 0)
+    out1 = dots(other, 1)
+    to_partner(0, out0)
+    out2 = dots(me_c, 0)
+    to_partner(1, out1)
 
     arrived(uX)
     for j in range(HZ):
@@ -456,15 +457,14 @@
         def _():
             z_copy(j, me_z).start()
 
-    moved_own(1)
+    out3 = dots(me_c, 1)
+    to_owners(0, out2)
+    to_owners(1, out3)
 
     sY = []
     for n in range(2):
-        for j in range(NY):
-            @pl.when(j != me_y)
-            def _():
-                tgt_copy(n, me_y, j).wait_recv()
-
+        for r in range(1, NY):
+            tgt_copy(n, r).wait_recv()
         sgb_ref[n, me_y] = add_up(sr_ref.at[n], NY)
         sY += exchange(lambda peer: sgb_ref.at[n, me_y], sgb_ref.at[n, me_y], me_y, NY, dev_y)
 
@@ -507,11 +507,8 @@
         copy.wait_send()
     for n in range(2):
         core_copy(n).wait_send()
-        for j in range(NY):
-            @pl.when(j != me_y)
-            def _():
-                tgt_copy(n, j, me_y).wait_send()
-
+        for r in range(1, NY):
+            tgt_copy(n, r).wait_send()
     for j in range(HZ):
         @pl.when(first_z + j != me_z)
         def _():
@@ -524,20 +521,16 @@
 
 def finish_kernel(*refs):
     n = len(refs) // 2
-    copies = [pltpu.make_async_copy(refs[i], refs[n + i], refs[-1].at[i]) for i in range(n)]
-    for copy in copies:
-        copy.start()
-    for copy in copies:
-        copy.wait()
+    for i in range(n):
+        refs[n + i][...] = refs[i][...]
 
 
 def finish(*arrays):
     return pl.pallas_call(
         finish_kernel,
         out_shape=tuple(jax.ShapeDtypeStruct(a.shape, a.dtype) for a in arrays),
-        in_specs=[pl.BlockSpec(memory_space=pl.ANY)] * len(arrays),
-        out_specs=[pl.BlockSpec(memory_space=pl.ANY)] * len(arrays),
-        scratch_shapes=[pltpu.SemaphoreType.DMA((len(arrays),))],
+        in_specs=[pl.BlockSpec(memory_space=pltpu.VMEM)] * len(arrays),
+        out_specs=[pl.BlockSpec(memory_space=pltpu.VMEM)] * len(arrays),
         compiler_params=pltpu.CompilerParams(vmem_limit_bytes=58 * 1024 * 1024),
         name="results",
     )(*arrays)

time: 76 us -> 68.3 us (0.90)
  Pallas kernels: 75 us -> 67.1 us
    pallas_call x1, Pallas kernels: 10.7 us -> 1.72 us  [finish(): pl.pallas_call(finish_kernel, out_shape=tuple((jax.ShapeDtypeStruct(a.sha...]
    pallas_call x1, Pallas kernels: 64.3 us -> 65.4 us  [local(): pl.pallas_call(functools.partial(kernel, dims), out_shape=(jax.ShapeDtype...]
where the time goes in v4:
time: 68.3 us; the launch traced here: 67.8 us
  Pallas kernels  67.1 us (98%)
    pallas_call x1, Pallas kernels, local(): pl.pallas_call(functools.partial(kernel, dims), out_shape=(jax.ShapeDtype...  65.4 us
    pallas_call x1, Pallas kernels, finish(): pl.pallas_call(finish_kernel, out_shape=tuple((jax.ShapeDtypeStruct(a.sha...  1.72 us

profile of v4, /device:TPU:1, one launch (start us, length us, event | category | flops | bytes accessed | tf_op | source)
XLA Modules:
  0.0 67.8 jit_solution(12502679113003469909)
XLA Ops:
  0.6 65.4 %sinkhorn.1 = (f32[8,128]{1,0:T(8,128)}, f32[32,128]{1,0:T(8,128)}, f32[64,1024]{1,0:T(8,128)}, f32[64,1,64]{2,1,0:T(1,128)}) custom-call(f32[64,1024]{1,0:T(8,128)} %x_ref.1, f32[64,4096]{1,0:T(8,128)} %y_hbm.1, f32[8,128]{1,0:T(8,128)} %bitcast.6, f32[32,128]{1,0:T(8,128)} %bitcast.4), custom_call_target="tpu_custom_call" | custom-call | flops 11274289152 | bytes 2621440 | tf_op jit(solution)/shard_map/sinkhorn/pallas_call | solution.py:549
  66.0 1.7 %results.1 = (f32[8,128]{1,0:T(8,128)}, f32[32,128]{1,0:T(8,128)}, f32[64,1024]{1,0:T(8,128)}, f32[64,1,64]{2,1,0:T(1,128)}) custom-call(f32[8,128]{1,0:T(8,128)} %get-tuple-element.12.refs_0_, f32[32,128]{1,0:T(8,128)} %get-tuple-element.13.refs_1_, f32[64,1024]{1,0:T(8,128)} %get-tuple-element.14.refs_2_, f32[64,1,64]{2,1,0:T(1,128)} %get-tuple-element.15.refs_3_), custom_call_target="tpu_custom_call" | custom-call | tf_op jit(solution)/shard_map/results/pallas_call | solution.py:529

commit v5 on v4

--- a/solution.py
+++ b/solution.py
@@ -85,16 +85,16 @@
         copy.wait_recv()
 
 
-def kernel(dims, x_ref, y_hbm, la_ref, lb_ref,
+def kernel(dims, x_hbm, y_hbm, la_ref, lb_ref,
            f_out, g_out, sg_out, tg_out,
            p_ref, hi_ref, lo_ref, xk_ref, yk_ref, mx_ref, sm_ref, vb_ref, cm_ref, mf_ref,
            xs_ref, las_ref, tmp_ref, run_ref, fc_ref, fm_ref, frc_ref, fr_ref, gm_ref, gx_ref, gz_ref, k_ref, w_ref,
            a_ref, xa_ref, yb_ref, cx_ref, cz_ref, d_ref, gs_ref,
            u_ref, r1_ref, t2_ref, r2_ref, tile_ref, so_ref, sc_ref, sy_ref, sr_ref, sgb_ref,
-           y_ref, send_sems, recv_sems, y_sems):
+           y_ref, f_ref, tg_ref, send_sems, recv_sems, y_sems, out_sems):
     NX, NZ, NY = dims
     NQ = 2 * NX
-    E, S = x_ref.shape
+    E, S = x_hbm.shape
     T = y_hbm.shape[1]
     T2, S2 = T // 2, 2 * S
     HZ = NZ // 2
@@ -126,8 +126,17 @@
         )
         for b in range(HZ)
     ]
+    load_x = pltpu.make_async_copy(x_hbm, xs_ref.at[me_c], y_sems.at[HZ])
+    load_x.start()
     for load in loads:
         load.start()
+
+    writes = []
+
+    def write(src_ref, out_ref):
+        copy = pltpu.make_async_copy(src_ref, out_ref, out_sems.at[len(writes)])
+        copy.start()
+        writes.append(copy)
 
     barrier = pltpu.get_barrier_semaphore()
     greeted = 0
@@ -188,7 +197,15 @@
             mx_ref[rows, :] = m
             sm_ref[rows, :] = acc
 
-    xs_ref[me_c] = x_ref[...]
+    def merge(h):
+        for i in range(SR):
+            rows = ds(h * S + i * L, L)
+            m = mx_ref[rows, :].T
+            top = jnp.max(m, 0, keepdims=True)
+            tmp_ref[0, pl.ds(h * SR + i, 1), :] = top
+            tmp_ref[1, pl.ds(h * SR + i, 1), :] = jnp.sum(sm_ref[rows, :].T * jnp.exp2(m - top), 0, keepdims=True)
+
+    load_x.wait()
     las_ref[me_c] = la_ref[...]
     prep_x(me_c)
     for load in loads:
@@ -198,7 +215,7 @@
     pl.semaphore_wait(barrier, greeted)
     base = sends.reserve(2)
     swap = [
-        sends.copy(x_ref, xs_ref.at[me_c], base, base, partner),
+        sends.copy(xs_ref.at[me_c], xs_ref.at[me_c], base, base, partner),
         sends.copy(la_ref, las_ref.at[me_c], base + 1, base + 1, partner),
     ]
     for copy in swap:
@@ -207,15 +224,11 @@
     scores(me_c, 1)
     arrived(swap)
     prep_x(other)
+    merge(me_c)
     scores(other, 0)
     scores(other, 1)
 
-    for i in range(NR):
-        rows = slice(i * L, (i + 1) * L)
-        m = mx_ref[rows, :].T
-        top = jnp.max(m, 0, keepdims=True)
-        tmp_ref[0, i:i + 1, :] = top
-        tmp_ref[1, i:i + 1, :] = jnp.sum(sm_ref[rows, :].T * jnp.exp2(m - top), 0, keepdims=True)
+    merge(other)
     fc_ref[me_c] = tmp_ref[0] + jnp.log2(tmp_ref[1])
     f1c = exchange(lambda peer: fc_ref.at[me_c], fc_ref.at[me_c], me_c, 2, dev_c)
 
@@ -333,9 +346,10 @@
     mine = lambda v: jnp.where(me_c == 0, v[0:SR], v[SR:NR])
     potential = (jnp.log2(total) - la2 + lse) / BETA
     for i in range(SR):
-        x = x_ref[:, i * L:(i + 1) * L]
+        x = xs_ref[me_c, :, i * L:(i + 1) * L]
         tmp_ref[1, i:i + 1, :] = jnp.sum(x * x, 0, keepdims=True) / E
-    f_out[...] = tmp_ref[1, 0:SR] - mine(potential)
+    f_ref[...] = tmp_ref[1, 0:SR] - mine(potential)
+    write(f_ref, f_out)
 
     for h in range(2):
         for i in range(SR):
@@ -436,8 +450,9 @@
     out0 = dots(other, 0)
     out1 = dots(other, 1)
     to_partner(0, out0)
+    to_partner(1, out1)
     out2 = dots(me_c, 0)
-    to_partner(1, out1)
+    to_owners(0, out2)
 
     arrived(uX)
     for j in range(HZ):
@@ -458,7 +473,6 @@
             z_copy(j, me_z).start()
 
     out3 = dots(me_c, 1)
-    to_owners(0, out2)
     to_owners(1, out3)
 
     sY = []
@@ -466,7 +480,8 @@
         for r in range(1, NY):
             tgt_copy(n, r).wait_recv()
         sgb_ref[n, me_y] = add_up(sr_ref.at[n], NY)
-        sY += exchange(lambda peer: sgb_ref.at[n, me_y], sgb_ref.at[n, me_y], me_y, NY, dev_y)
+        sY.append(exchange(lambda peer: sgb_ref.at[n, me_y], sgb_ref.at[n, me_y], me_y, NY, dev_y))
+        write(sgb_ref.at[n, me_y], sg_out.at[:, ds(me_y * RB + n * RH, RH)])
 
     tile_base = sends.reserve(1)
     tile_copy = sends.copy(tile_ref, tile_ref, tile_base, tile_base, partner)
@@ -492,17 +507,21 @@
         tile_copy.wait_recv()
 
     tile = tile_ref[...]
-    tg_out[:, 0, :] = jnp.where(me_c == 0, tile[:, 0:E], tile[:, E:2 * E])
+    tg_ref[:, 0, :] = jnp.where(me_c == 0, tile[:, 0:E], tile[:, E:2 * E])
+    write(tg_ref, tg_out)
 
     arrived(gC)
-    g_out[0:NT] = gs_ref[0]
-    g_out[NT:2 * NT] = gs_ref[1]
-
-    arrived(sY)
+    for j in range(2):
+        write(gs_ref.at[j], g_out.at[j * NT:(j + 1) * NT])
+
     for n in range(2):
-        for j in range(NY):
-            sg_out[:, j * RB + n * RH:j * RB + (n + 1) * RH] = sgb_ref[n, j]
-
+        for r in range(1, NY):
+            sY[n][r - 1].wait_recv()
+            j = lax.rem(me_y + NY - r, NY)
+            write(sgb_ref.at[n, j], sg_out.at[:, ds(j * RB + n * RH, RH)])
+
+    for copy in writes:
+        copy.wait()
     for copy in sends.live:
         copy.wait_send()
     for n in range(2):
@@ -554,8 +573,8 @@
             jax.ShapeDtypeStruct((E, S), F32),
             jax.ShapeDtypeStruct((E, 1, 64), F32),
         ),
-        in_specs=[pl.BlockSpec(memory_space=pl.ANY if i == 1 else pltpu.VMEM) for i in range(4)],
-        out_specs=[pl.BlockSpec(memory_space=pltpu.VMEM)] * 4,
+        in_specs=[pl.BlockSpec(memory_space=pl.ANY if i < 2 else pltpu.VMEM) for i in range(4)],
+        out_specs=[pl.BlockSpec(memory_space=pl.ANY)] * 4,
         scratch_shapes=[
             vmem((S2, T2)), vmem((S2, T2), BF16), vmem((S2, T2), BF16),
             vmem((S2, 8 * E), BF16), vmem((8 * E, T2), BF16),
@@ -569,8 +588,9 @@
             vmem((NX, HZ, E, L)), vmem((NX, HZ, E, L)), vmem((HZ, E, L)), vmem((NZ, E, L)), vmem((E, L)),
             vmem((2, NY, E, RB // 2)), vmem((2, NY, E, RB // 2)),
             vmem((2, NY, E, RB // 2)), vmem((2, NY, E, RB // 2)), vmem((2, NY, E, RB // 2)),
-            vmem((E, T2)),
-            pltpu.SemaphoreType.DMA((n_sems,)), pltpu.SemaphoreType.DMA((n_sems,)), pltpu.SemaphoreType.DMA((HZ,)),
+            vmem((E, T2)), vmem((SR, L)), vmem((E, 1, 64)),
+            pltpu.SemaphoreType.DMA((n_sems,)), pltpu.SemaphoreType.DMA((n_sems,)), pltpu.SemaphoreType.DMA((HZ + 1,)),
+            pltpu.SemaphoreType.DMA((4 + 2 * NY,)),
         ],
         compiler_params=pltpu.CompilerParams(
             collective_id=0, has_side_effects=True, vmem_limit_bytes=58 * 1024 * 1024

time: 68.3 us -> 67.2 us (0.984)
  Pallas kernels: 67.1 us -> 66.1 us
    pallas_call x1, Pallas kernels: 65.4 us -> 64.4 us  [local(): pl.pallas_call(functools.partial(kernel, dims), out_shape=(jax.ShapeDtype...]
where the time goes in v5:
time: 67.2 us; the launch traced here: 66.7 us
  Pallas kernels  66.1 us (98%)
    pallas_call x1, Pallas kernels, local(): pl.pallas_call(functools.partial(kernel, dims), out_shape=(jax.ShapeDtype...  64.4 us
    pallas_call x1, Pallas kernels, finish(): pl.pallas_call(finish_kernel, out_shape=tuple((jax.ShapeDtypeStruct(a.sha...  1.72 us

profile of v5, /device:TPU:1, one launch (start us, length us, event | category | flops | bytes accessed | tf_op | source)
XLA Modules:
  0.0 66.7 jit_solution(320895107956095049)
XLA Ops:
  0.6 64.4 %sinkhorn.1 = (f32[8,128]{1,0:T(8,128)}, f32[32,128]{1,0:T(8,128)}, f32[64,1024]{1,0:T(8,128)}, f32[64,1,64]{2,1,0:T(1,128)}) custom-call(f32[64,1024]{1,0:T(8,128)} %x_hbm.1, f32[64,4096]{1,0:T(8,128)} %y_hbm.1, f32[8,128]{1,0:T(8,128)} %bitcast.6, f32[32,128]{1,0:T(8,128)} %bitcast.4), custom_call_target="tpu_custom_call" | custom-call | flops 11274289152 | bytes 2621440 | tf_op jit(solution)/shard_map/sinkhorn/pallas_call | solution.py:568
  65.0 1.7 %results.1 = (f32[8,128]{1,0:T(8,128)}, f32[32,128]{1,0:T(8,128)}, f32[64,1024]{1,0:T(8,128)}, f32[64,1,64]{2,1,0:T(1,128)}) custom-call(f32[8,128]{1,0:T(8,128)} %get-tuple-element.12.refs_0_, f32[32,128]{1,0:T(8,128)} %get-tuple-element.13.refs_1_, f32[64,1024]{1,0:T(8,128)} %get-tuple-element.14.refs_2_, f32[64,1,64]{2,1,0:T(1,128)} %get-tuple-element.15.refs_3_), custom_call_target="tpu_custom_call" | custom-call | tf_op jit(solution)/shard_map/results/pallas_call | solution.py:548

commit v6 on v5

--- a/solution.py
+++ b/solution.py
@@ -48,6 +48,10 @@
     return total
 
 
+def far_first(n):
+    return sorted(range(1, n), key=lambda r: -min(r, n - r))
+
+
 class Sends:
     def __init__(self, send_sems, recv_sems):
         self.send_sems, self.recv_sems = send_sems, recv_sems
@@ -74,8 +78,8 @@
         for r in range(1, n):
             peer = lax.rem(me + r, n)
             copies.append(self.copy(src(peer), dst, base + r - 1, base + r - 1, device(peer)))
-        for copy in copies:
-            copy.start()
+        for r in far_first(n):
+            copies[r - 1].start()
         self.live += copies
         return copies
 
@@ -126,24 +130,24 @@
         )
         for b in range(HZ)
     ]
+    writes = []
+
+    def write(src_ref, out_ref):
+        copy = pltpu.make_async_copy(src_ref, out_ref, out_sems.at[len(writes)])
+        copy.start()
+        writes.append(copy)
+
+    barrier = pltpu.get_barrier_semaphore()
+    greeted = 0
+    for me, n, device in ((me_z, NZ, dev_z), (me_x, NX, dev_x), (me_y, NY, dev_y), (me_c, 2, dev_c)):
+        for r in far_first(n):
+            pl.semaphore_signal(barrier, inc=1, device_id=device(lax.rem(me + r, n)), device_id_type=MESH)
+            greeted += 1
+
     load_x = pltpu.make_async_copy(x_hbm, xs_ref.at[me_c], y_sems.at[HZ])
     load_x.start()
     for load in loads:
         load.start()
-
-    writes = []
-
-    def write(src_ref, out_ref):
-        copy = pltpu.make_async_copy(src_ref, out_ref, out_sems.at[len(writes)])
-        copy.start()
-        writes.append(copy)
-
-    barrier = pltpu.get_barrier_semaphore()
-    greeted = 0
-    for me, n, device in ((me_c, 2, dev_c), (me_y, NY, dev_y), (me_x, NX, dev_x), (me_z, NZ, dev_z)):
-        for r in range(1, n):
-            pl.semaphore_signal(barrier, inc=1, device_id=device(lax.rem(me + r, n)), device_id_type=MESH)
-            greeted += 1
 
     def prep_y(b, _):
         cols = ds(b * CB, CB)
@@ -444,7 +448,7 @@
                 sr_ref[n, me_y] = term
             else:
                 sy_ref[n, r] = term
-        for r in range(1, NY):
+        for r in far_first(NY):
             tgt_copy(n, r).start()
 
     out0 = dots(other, 0)

time: 67.2 us -> 65.9 us (0.981)
  Pallas kernels: 66.1 us -> 64.8 us
    pallas_call x1, Pallas kernels: 64.4 us -> 63 us  [local(): pl.pallas_call(functools.partial(kernel, dims), out_shape=(jax.ShapeDtype...]
where the time goes in v6:
time: 65.9 us; the launch traced here: 65.4 us
  Pallas kernels  64.8 us (98%)
    pallas_call x1, Pallas kernels, local(): pl.pallas_call(functools.partial(kernel, dims), out_shape=(jax.ShapeDtype...  63 us
    pallas_call x1, Pallas kernels, finish(): pl.pallas_call(finish_kernel, out_shape=tuple((jax.ShapeDtypeStruct(a.sha...  1.72 us

profile of v6, /device:TPU:1, one launch (start us, length us, event | category | flops | bytes accessed | tf_op | source)
XLA Modules:
  0.0 65.4 jit_solution(2313146306207698387)
XLA Ops:
  0.6 63.0 %sinkhorn.1 = (f32[8,128]{1,0:T(8,128)}, f32[32,128]{1,0:T(8,128)}, f32[64,1024]{1,0:T(8,128)}, f32[64,1,64]{2,1,0:T(1,128)}) custom-call(f32[64,1024]{1,0:T(8,128)} %x_hbm.1, f32[64,4096]{1,0:T(8,128)} %y_hbm.1, f32[8,128]{1,0:T(8,128)} %bitcast.6, f32[32,128]{1,0:T(8,128)} %bitcast.4), custom_call_target="tpu_custom_call" | custom-call | flops 11274289152 | bytes 2621440 | tf_op jit(solution)/shard_map/sinkhorn/pallas_call | solution.py:572
  63.7 1.7 %results.1 = (f32[8,128]{1,0:T(8,128)}, f32[32,128]{1,0:T(8,128)}, f32[64,1024]{1,0:T(8,128)}, f32[64,1,64]{2,1,0:T(1,128)}) custom-call(f32[8,128]{1,0:T(8,128)} %get-tuple-element.12.refs_0_, f32[32,128]{1,0:T(8,128)} %get-tuple-element.13.refs_1_, f32[64,1024]{1,0:T(8,128)} %get-tuple-element.14.refs_2_, f32[64,1,64]{2,1,0:T(1,128)} %get-tuple-element.15.refs_3_), custom_call_target="tpu_custom_call" | custom-call | tf_op jit(solution)/shard_map/results/pallas_call | solution.py:552

commit v7 on v6

--- a/solution.py
+++ b/solution.py
@@ -400,9 +400,6 @@
 
     lax.fori_loop(0, HZ, prep_b, 0)
 
-    gs_ref[me_c] = (LOG2E * b_mine - g_lse - jnp.log2(d)) / BETA
-    gC = exchange(lambda peer: gs_ref.at[me_c], gs_ref.at[me_c], me_c, 2, dev_c)
-
     core_base = sends.reserve(2)
     tgt_base = sends.reserve(2 * NY)
     RH = RB // 2
@@ -478,6 +475,10 @@
 
     out3 = dots(me_c, 1)
     to_owners(1, out3)
+
+    gs_ref[me_c] = (LOG2E * b_mine - g_lse - jnp.log2(d)) / BETA
+    gC = exchange(lambda peer: gs_ref.at[me_c], gs_ref.at[me_c], me_c, 2, dev_c)
+
 
     sY = []
     for n in range(2):

time: 65.9 us -> 65.9 us (level)
  no operation moved by 1% of the time
where the time goes in v7:
time: 65.9 us; the launch traced here: 65.4 us
  Pallas kernels  64.8 us (98%)
    pallas_call x1, Pallas kernels, local(): pl.pallas_call(functools.partial(kernel, dims), out_shape=(jax.ShapeDtype...  63.1 us
    pallas_call x1, Pallas kernels, finish(): pl.pallas_call(finish_kernel, out_shape=tuple((jax.ShapeDtypeStruct(a.sha...  1.72 us

profile of v7, /device:TPU:1, one launch (start us, length us, event | category | flops | bytes accessed | tf_op | source)
XLA Modules:
  0.0 65.4 jit_solution(7402119068048850202)
XLA Ops:
  0.6 63.1 %sinkhorn.1 = (f32[8,128]{1,0:T(8,128)}, f32[32,128]{1,0:T(8,128)}, f32[64,1024]{1,0:T(8,128)}, f32[64,1,64]{2,1,0:T(1,128)}) custom-call(f32[64,1024]{1,0:T(8,128)} %x_hbm.1, f32[64,4096]{1,0:T(8,128)} %y_hbm.1, f32[8,128]{1,0:T(8,128)} %bitcast.6, f32[32,128]{1,0:T(8,128)} %bitcast.4), custom_call_target="tpu_custom_call" | custom-call | flops 11274289152 | bytes 2621440 | tf_op jit(solution)/shard_map/sinkhorn/pallas_call | solution.py:573
  63.7 1.7 %results.1 = (f32[8,128]{1,0:T(8,128)}, f32[32,128]{1,0:T(8,128)}, f32[64,1024]{1,0:T(8,128)}, f32[64,1,64]{2,1,0:T(1,128)}) custom-call(f32[8,128]{1,0:T(8,128)} %get-tuple-element.12.refs_0_, f32[32,128]{1,0:T(8,128)} %get-tuple-element.13.refs_1_, f32[64,1024]{1,0:T(8,128)} %get-tuple-element.14.refs_2_, f32[64,1,64]{2,1,0:T(1,128)} %get-tuple-element.15.refs_3_), custom_call_target="tpu_custom_call" | custom-call | tf_op jit(solution)/shard_map/results/pallas_call | solution.py:553
